TPU v7x, 32 devices: a whole 2x2x4 slice. The times are simulated.
32 devices in a mesh: seq: 8 (over z, x), fsdp: 4 (over y, core).
Axes of the slice: x: 2, y: 2, z: 4, core: 2. Of those that a mesh axis runs over, the one named last changes fastest.
Arguments:
- tokens: bfloat16 [4, 8192, 1024], P('fsdp', 'seq'), may hold values from -6 to 6
- cotangent: bfloat16 [4, 8192, 1024], P('fsdp', 'seq'), may hold values from -6 to 6
- lengths: int32 [4], P('fsdp'), may hold values from 2048 to 8192, as said below
- triple_weight: float32 [1024, 3072], P('seq', 'fsdp'), may hold values from -0.1875 to 0.1875
- output_weight: float32 [1024, 1024], P('seq', 'fsdp'), may hold values from -6 to 6
- expand_weight: float32 [1024, 5248], P('seq', 'fsdp'), may hold values from -0.1875 to 0.1875
- shrink_weight: float32 [2624, 1024], P('fsdp', 'seq'), may hold values from -0.125 to 0.125
- norm_gains: float32 [2, 1024], replicated, may hold values from 0.5 to 1.5
- side_bases: float32 [4, 1024, 1024], P(None, 'seq'), may hold values from -1 to 1, as said below
- output_right: float32 [1024, 1024], P('fsdp'), may hold values from -1 to 1, as said below
- triple_first: float32 [1024, 3072], P('seq', 'fsdp'), may hold values from -28 to 28
- triple_second: float32 [1024, 3072], P('seq', 'fsdp'), may hold values from 409.6 to 1638.4
- output_first: float32 [1024, 1024], P('seq', 'fsdp'), may hold values from -2.5 to 2.5
- output_second: float32 [1024, 1024], P('seq', 'fsdp'), may hold values from 0.52 to 2
- expand_first: float32 [1024, 5248], P('seq', 'fsdp'), may hold values from -16 to 16
- expand_second: float32 [1024, 5248], P('seq', 'fsdp'), may hold values from 147.456 to 589.824
- shrink_first: float32 [2624, 1024], P('fsdp', 'seq'), may hold values from -28 to 28
- shrink_second: float32 [2624, 1024], P('fsdp', 'seq'), may hold values from 409.6 to 1638.4
- gains_first: float32 [2, 1024], replicated, may hold values from -32 to 32
- gains_second: float32 [2, 1024], replicated, may hold values from 589.824 to 2359.296
Outputs:
- mixed: bfloat16 [4, 8192, 1024], P('fsdp', 'seq')
- token_gradient: bfloat16 [4, 8192, 1024], P('fsdp', 'seq')
- triple_gradient: float32 [1024, 3072], P('seq', 'fsdp')
- output_gradient: float32 [1024, 1024], P('seq', 'fsdp')
- expand_gradient: float32 [1024, 5248], P('seq', 'fsdp')
- shrink_gradient: float32 [2624, 1024], P('fsdp', 'seq')
- gains_gradient: float32 [2, 1024], replicated
- triple_average: float32 [1024, 3072], P('seq', 'fsdp')
- triple_variance: float32 [1024, 3072], P('seq', 'fsdp')
- triple_updated: float32 [1024, 3072], P('seq', 'fsdp')
- triple_copy: bfloat16 [1024, 3072], P('seq', 'fsdp')
- output_average: float32 [1024, 1024], P('seq', 'fsdp')
- output_variance: float32 [1024, 1024], P('seq', 'fsdp')
- output_updated: float32 [1024, 1024], P('seq', 'fsdp')
- output_copy: bfloat16 [1024, 1024], P('seq', 'fsdp')
- expand_average: float32 [1024, 5248], P('seq', 'fsdp')
- expand_variance: float32 [1024, 5248], P('seq', 'fsdp')
- expand_updated: float32 [1024, 5248], P('seq', 'fsdp')
- expand_copy: bfloat16 [1024, 5248], P('seq', 'fsdp')
- shrink_average: float32 [2624, 1024], P('fsdp', 'seq')
- shrink_variance: float32 [2624, 1024], P('fsdp', 'seq')
- shrink_updated: float32 [2624, 1024], P('fsdp', 'seq')
- shrink_copy: bfloat16 [2624, 1024], P('fsdp', 'seq')
- gains_average: float32 [2, 1024], replicated
- gains_variance: float32 [2, 1024], replicated
- gains_updated: float32 [2, 1024], replicated
Inputs may be any that keep to these rules, and one draw needn't show every extreme that they name: Row r holds one sequence in its first lengths[r] slots, the rest is padding; some row is full. `side_bases`: each of the four matrices is orthogonal. `output_right`: orthogonal.
All inputs are finite; a program needn't handle non-finite values.
Results may differ from a plain program's by a relative error of at most 0.028.
Values may be sent and summed in bfloat16 or wider, within the bound.
No kernel may reach another device: no remote copies, remote signals or barrier semaphores. Data moves between devices by JAX's collectives and lax.ppermute only.
A program may use at most 448 MiB of HBM per device.

v0:
```python
import jax
import jax.numpy as jnp
from jax import lax
from jax.sharding import PartitionSpec as P

HEADS = 16
HEAD_DIM = 64
FF = 2624
STEP = 10


ROPE_BASE = 160000.0
NORM_EPS = 1e-05
NEG_LARGE = -1e30
BETA_ONE = 0.95
BETA_TWO = 0.95
ADAM_EPS = 1e-08
DECAY_RATE = 0.01
WEIGHT_RATES = (0.03, 1.0, 0.03, 0.03)
GAINS_RATE = 0.8


def layer_norm(values, gain):
    centre = values - jnp.mean(values, axis=-1, keepdims=True)
    spread = jnp.mean(centre * centre, axis=-1, keepdims=True)
    return centre * lax.rsqrt(spread + NORM_EPS) * gain


def rotary_tables(position, head_size):
    halves = head_size // 2
    frequency = ROPE_BASE ** (-2.0 * jnp.arange(halves, dtype=jnp.float32) / head_size)
    angle = position.astype(jnp.float32)[:, None] * frequency[None, :]
    return (
        jnp.concatenate([jnp.cos(angle), jnp.cos(angle)], -1),
        jnp.concatenate([jnp.sin(angle), jnp.sin(angle)], -1),
    )


def turn(values, cosine, sine):
    halves = values.shape[-1] // 2
    rolled = jnp.concatenate([-values[..., halves:], values[..., :halves]], -1)
    return values * cosine[:, None, :] + rolled * sine[:, None, :]


def turn_back(values, cosine, sine):
    halves = values.shape[-1] // 2
    scaled = values * sine[:, None, :]
    return values * cosine[:, None, :] + jnp.concatenate(
        [scaled[..., halves:], -scaled[..., :halves]], -1
    )


def gated(inner):
    return jax.nn.gelu(inner[:, :FF], approximate=False) * inner[:, FF:]


def outer_sum(left, right):
    return lax.dot_general(
        left, right, (((0,), (0,)), ((), ())), preferred_element_type=jnp.float32
    )


def back_product(left, right):
    return lax.dot_general(
        left, right, (((1,), (1,)), ((), ())), preferred_element_type=jnp.float32
    )


def plain_product(left, right):
    return jnp.dot(left, right, preferred_element_type=jnp.float32)


def masked_scores(query_part, key_part, key_start, lengths):
    scores = jnp.einsum(
        "rqhd,rkhd->rqhk", query_part, key_part, preferred_element_type=jnp.float32
    ) * HEAD_DIM ** (-0.5)
    places = key_start + jnp.arange(key_part.shape[1], dtype=jnp.int32)
    usable = places[None, :] < lengths[:, None]
    return jnp.where(usable[:, None, None, :], scores, NEG_LARGE)


def shared_terms(
    query_part, back_part, key_part, value_part, key_start, lengths, log_part, balance_part
):
    scores = masked_scores(query_part, key_part, key_start, lengths)
    chance = jnp.exp(scores - log_part[..., None])
    chance_back = jnp.einsum(
        "rqhd,rkhd->rqhk", back_part, value_part, preferred_element_type=jnp.float32
    )
    score_back = (chance * (chance_back - balance_part[..., None])).astype(jnp.bfloat16)
    return (chance.astype(jnp.bfloat16), score_back)


def in_blocks(step, carry, piece, block):
    length = piece[0].shape[1]
    size = min(length, block)
    count = length // size

    def inner_step(state, index):
        part = tuple((lax.dynamic_slice_in_dim(member, index * size, size, 1) for member in piece))
        return (step(state, part, index * size), None)

    state, unused = lax.scan(inner_step, carry, jnp.arange(count, dtype=jnp.int32))
    return state


def adam_step(rotated, first, second):
    average = BETA_ONE * first + (1.0 - BETA_ONE) * rotated
    variance = BETA_TWO * second + (1.0 - BETA_TWO) * rotated * rotated
    direction = (
        average / (1.0 - BETA_ONE**STEP) / (jnp.sqrt(variance / (1.0 - BETA_TWO**STEP)) + ADAM_EPS)
    )
    return (average, variance, direction)


def body(
    tokens,
    cotangent,
    lengths,
    triple_weight,
    output_weight,
    expand_weight,
    shrink_weight,
    norm_gains,
    side_bases,
    output_right,
    triple_first,
    triple_second,
    output_first,
    output_second,
    expand_first,
    expand_second,
    shrink_first,
    shrink_second,
    gains_first,
    gains_second,
):
    rows_here, local_len, width = tokens.shape
    count = rows_here * local_len
    key_block = max(512, local_len)
    offset = lax.axis_index("seq") * local_len
    position = offset + jnp.arange(local_len, dtype=jnp.int32)
    cosine, sine = rotary_tables(position, HEAD_DIM)
    cosine = jnp.tile(cosine, (rows_here, 1))
    sine = jnp.tile(sine, (rows_here, 1))
    valid = (position[None, :] < lengths[:, None]).astype(jnp.float32).reshape(count, 1)
    shape_heads = (rows_here, local_len, HEADS, HEAD_DIM)
    wide = (
        lax.all_gather(triple_weight.astype(jnp.bfloat16), "fsdp", axis=1, tiled=True),
        lax.all_gather(output_weight.astype(jnp.bfloat16), "fsdp", axis=1, tiled=True),
        lax.all_gather(expand_weight.astype(jnp.bfloat16), "fsdp", axis=1, tiled=True),
        lax.all_gather(shrink_weight.astype(jnp.bfloat16), "fsdp", axis=0, tiled=True),
    )
    whole = (
        lax.all_gather(wide[0], "seq", axis=0, tiled=True),
        lax.all_gather(wide[1], "seq", axis=0, tiled=True),
        lax.all_gather(wide[2], "seq", axis=0, tiled=True),
        lax.all_gather(wide[3], "seq", axis=1, tiled=True),
    )
    full_triple, full_output, full_expand, full_shrink = whole
    flat = tokens.reshape(count, width).astype(jnp.float32)
    first_normed, first_back = jax.vjp(layer_norm, flat, norm_gains[0])
    first_low = first_normed.astype(jnp.bfloat16)
    joint = jnp.dot(first_low, full_triple, preferred_element_type=jnp.float32)
    query_heads = (
        turn(joint[:, :width].reshape(count, HEADS, HEAD_DIM), cosine, sine)
        .astype(jnp.bfloat16)
        .reshape(shape_heads)
    )
    key_heads = (
        turn(joint[:, width : 2 * width].reshape(count, HEADS, HEAD_DIM), cosine, sine)
        .astype(jnp.bfloat16)
        .reshape(shape_heads)
    )
    value_heads = joint[:, 2 * width :].astype(jnp.bfloat16).reshape(shape_heads)
    flat_keys = key_heads.reshape(rows_here, local_len, width)
    flat_values = value_heads.reshape(rows_here, local_len, width)

    def forward_piece(carry, piece, start):
        total, peak, mass = carry
        size = piece[0].shape[1]
        key_part = piece[0].reshape(rows_here, size, HEADS, HEAD_DIM)
        value_part = piece[1].reshape(rows_here, size, HEADS, HEAD_DIM)
        scores = masked_scores(query_heads, key_part, start, lengths)
        new_peak = jnp.maximum(peak, jnp.max(scores, axis=-1))
        factor = jnp.exp(peak - new_peak)
        weights = jnp.exp(scores - new_peak[..., None])
        mass = mass * factor + jnp.sum(weights, axis=-1)
        total = total * factor[..., None] + jnp.einsum(
            "rqhk,rkhd->rqhd",
            weights.astype(jnp.bfloat16),
            value_part,
            preferred_element_type=jnp.float32,
        )
        return (total, new_peak, mass)

    stats_shape = (rows_here, local_len, HEADS)
    start_state = (
        jnp.zeros(shape_heads, jnp.float32),
        jnp.full(stats_shape, NEG_LARGE, jnp.float32),
        jnp.zeros(stats_shape, jnp.float32),
    )
    total, peak, mass = in_blocks(
        forward_piece,
        start_state,
        (
            lax.all_gather(flat_keys, "seq", axis=1, tiled=True),
            lax.all_gather(flat_values, "seq", axis=1, tiled=True),
        ),
        key_block,
    )
    attend = total / mass[..., None]
    log_mass = peak + jnp.log(mass)
    attend_low = attend.reshape(count, width).astype(jnp.bfloat16)
    branch = jnp.dot(attend_low, full_output, preferred_element_type=jnp.float32)
    middle = flat + branch
    second_normed, second_back = jax.vjp(layer_norm, middle, norm_gains[1])
    second_low = second_normed.astype(jnp.bfloat16)
    inner = jnp.dot(second_low, full_expand, preferred_element_type=jnp.float32)
    hidden, gated_back = jax.vjp(gated, inner)
    hidden_low = hidden.astype(jnp.bfloat16)
    shrunk = jnp.dot(hidden_low, full_shrink, preferred_element_type=jnp.float32)
    mixed = ((middle + shrunk) * valid).astype(jnp.bfloat16).reshape(tokens.shape)
    upstream = cotangent.reshape(count, width).astype(jnp.float32) * valid
    upstream_low = upstream.astype(jnp.bfloat16)
    shrink_part = outer_sum(hidden_low, upstream_low)
    inner_back = gated_back(back_product(upstream_low, full_shrink))[0].astype(jnp.bfloat16)
    expand_part = outer_sum(second_low, inner_back)
    second_input, second_gain = second_back(back_product(inner_back, full_expand))
    middle_back = upstream + second_input
    branch_low = middle_back.astype(jnp.bfloat16)
    output_part = outer_sum(attend_low, branch_low)
    attend_back = back_product(branch_low, full_output).astype(jnp.bfloat16)
    attend_heads = attend_back.reshape(shape_heads)
    balance = jnp.sum(attend_heads.astype(jnp.float32) * attend, axis=-1)

    def summed_piece(carry, piece, start):
        query_sum, key_store, value_store = carry
        size = piece[0].shape[1]
        key_part = piece[0].reshape(rows_here, size, HEADS, HEAD_DIM)
        value_part = piece[1].reshape(rows_here, size, HEADS, HEAD_DIM)
        chance_low, score_back = shared_terms(
            query_heads, attend_heads, key_part, value_part, start, lengths, log_mass, balance
        )
        query_sum = query_sum + jnp.einsum(
            "rqhk,rkhd->rqhd", score_back, key_part, preferred_element_type=jnp.float32
        )
        key_piece = jnp.einsum(
            "rqhk,rqhd->rkhd", score_back, query_heads, preferred_element_type=jnp.float32
        ).reshape(rows_here, size, width)
        value_piece = jnp.einsum(
            "rqhk,rqhd->rkhd", chance_low, attend_heads, preferred_element_type=jnp.float32
        ).reshape(rows_here, size, width)
        key_store = lax.dynamic_update_slice_in_dim(key_store, key_piece, start, 1)
        value_store = lax.dynamic_update_slice_in_dim(value_store, value_piece, start, 1)
        return (query_sum, key_store, value_store)

    total_len = local_len * lax.axis_size("seq")
    query_zero = jnp.zeros(shape_heads, jnp.float32)
    back_init = (
        query_zero,
        jnp.zeros((rows_here, total_len, width), jnp.float32),
        jnp.zeros((rows_here, total_len, width), jnp.float32),
    )
    back_result = in_blocks(
        summed_piece,
        back_init,
        (
            lax.all_gather(flat_keys, "seq", axis=1, tiled=True),
            lax.all_gather(flat_values, "seq", axis=1, tiled=True),
        ),
        key_block,
    )
    query_grad = back_result[0]
    key_grad, value_grad = (
        lax.psum_scatter(
            back_result[1].astype(jnp.bfloat16), "seq", scatter_dimension=1, tiled=True
        ).astype(jnp.float32),
        lax.psum_scatter(
            back_result[2].astype(jnp.bfloat16), "seq", scatter_dimension=1, tiled=True
        ).astype(jnp.float32),
    )
    scale = HEAD_DIM ** (-0.5)
    query_grad = query_grad.reshape(count, HEADS, HEAD_DIM) * scale
    key_grad = key_grad.reshape(count, HEADS, HEAD_DIM) * scale
    joint_back = jnp.concatenate(
        [
            turn_back(query_grad, cosine, sine).reshape(count, width),
            turn_back(key_grad, cosine, sine).reshape(count, width),
            value_grad.reshape(count, width),
        ],
        axis=1,
    ).astype(jnp.bfloat16)
    triple_part = outer_sum(first_low, joint_back)
    first_input, first_gain = first_back(back_product(joint_back, full_triple))
    token_gradient = (middle_back + first_input).astype(jnp.bfloat16).reshape(tokens.shape)
    partly_summed = (
        lax.psum_scatter(
            triple_part.astype(jnp.bfloat16), "seq", scatter_dimension=0, tiled=True
        ).astype(jnp.float32),
        lax.psum_scatter(
            output_part.astype(jnp.bfloat16), "seq", scatter_dimension=0, tiled=True
        ).astype(jnp.float32),
        lax.psum_scatter(
            expand_part.astype(jnp.bfloat16), "seq", scatter_dimension=0, tiled=True
        ).astype(jnp.float32),
        lax.psum_scatter(
            shrink_part.astype(jnp.bfloat16), "seq", scatter_dimension=1, tiled=True
        ).astype(jnp.float32),
    )
    owned = (
        lax.psum_scatter(
            partly_summed[0].astype(jnp.bfloat16), "fsdp", scatter_dimension=1, tiled=True
        ).astype(jnp.float32),
        lax.psum_scatter(
            partly_summed[1].astype(jnp.bfloat16), "fsdp", scatter_dimension=1, tiled=True
        ).astype(jnp.float32),
        lax.psum_scatter(
            partly_summed[2].astype(jnp.bfloat16), "fsdp", scatter_dimension=1, tiled=True
        ).astype(jnp.float32),
        lax.psum_scatter(
            partly_summed[3].astype(jnp.bfloat16), "fsdp", scatter_dimension=0, tiled=True
        ).astype(jnp.float32),
    )
    gains_gradient = lax.psum(jnp.stack([first_gain, second_gain]), ("seq", "fsdp"))
    triple_gradient, output_gradient, expand_gradient, shrink_gradient = owned
    bases_low = side_bases.astype(jnp.bfloat16)
    right_low = output_right.astype(jnp.bfloat16)
    turned = (
        lax.psum_scatter(
            outer_sum(bases_low[0], triple_gradient.astype(jnp.bfloat16)).astype(jnp.bfloat16),
            "seq",
            scatter_dimension=0,
            tiled=True,
        ).astype(jnp.float32),
        lax.psum_scatter(
            outer_sum(bases_low[1], output_gradient.astype(jnp.bfloat16)).astype(jnp.bfloat16),
            "seq",
            scatter_dimension=0,
            tiled=True,
        ).astype(jnp.float32),
        lax.psum_scatter(
            outer_sum(bases_low[2], expand_gradient.astype(jnp.bfloat16)).astype(jnp.bfloat16),
            "seq",
            scatter_dimension=0,
            tiled=True,
        ).astype(jnp.float32),
        lax.psum_scatter(
            plain_product(shrink_gradient.astype(jnp.bfloat16), bases_low[3]).astype(jnp.bfloat16),
            "seq",
            scatter_dimension=1,
            tiled=True,
        ).astype(jnp.float32),
    )
    output_turned = lax.psum_scatter(
        plain_product(turned[1].astype(jnp.bfloat16), right_low).astype(jnp.bfloat16),
        "fsdp",
        scatter_dimension=1,
        tiled=True,
    ).astype(jnp.float32)
    triple_average, triple_variance, triple_direction = adam_step(
        turned[0], triple_first, triple_second
    )
    output_average, output_variance, output_direction = adam_step(
        output_turned, output_first, output_second
    )
    expand_average, expand_variance, expand_direction = adam_step(
        turned[2], expand_first, expand_second
    )
    shrink_average, shrink_variance, shrink_direction = adam_step(
        turned[3], shrink_first, shrink_second
    )
    gains_average, gains_variance, gains_direction = adam_step(
        gains_gradient, gains_first, gains_second
    )
    output_wide = lax.all_gather(output_direction.astype(jnp.bfloat16), "fsdp", axis=1, tiled=True)
    output_middle = back_product(output_wide, right_low).astype(jnp.bfloat16)
    backs = (
        lax.all_gather(triple_direction.astype(jnp.bfloat16), "seq", axis=0, tiled=True),
        lax.all_gather(output_middle, "seq", axis=0, tiled=True),
        lax.all_gather(expand_direction.astype(jnp.bfloat16), "seq", axis=0, tiled=True),
        lax.all_gather(shrink_direction.astype(jnp.bfloat16), "seq", axis=1, tiled=True),
    )
    triple_back = plain_product(bases_low[0], backs[0])
    output_back = plain_product(bases_low[1], backs[1])
    expand_back = plain_product(bases_low[2], backs[2])
    shrink_back = back_product(backs[3], bases_low[3])
    triple_updated = (triple_weight - WEIGHT_RATES[0] * triple_back) * (
        1.0 - WEIGHT_RATES[0] * DECAY_RATE
    )
    output_updated = (output_weight - WEIGHT_RATES[1] * output_back) * (
        1.0 - WEIGHT_RATES[1] * DECAY_RATE
    )
    expand_updated = (expand_weight - WEIGHT_RATES[2] * expand_back) * (
        1.0 - WEIGHT_RATES[2] * DECAY_RATE
    )
    shrink_updated = (shrink_weight - WEIGHT_RATES[3] * shrink_back) * (
        1.0 - WEIGHT_RATES[3] * DECAY_RATE
    )
    gains_updated = norm_gains - GAINS_RATE * gains_direction
    return (
        mixed,
        token_gradient,
        triple_gradient,
        output_gradient,
        expand_gradient,
        shrink_gradient,
        gains_gradient,
        triple_average,
        triple_variance,
        triple_updated,
        triple_updated.astype(jnp.bfloat16),
        output_average,
        output_variance,
        output_updated,
        output_updated.astype(jnp.bfloat16),
        expand_average,
        expand_variance,
        expand_updated,
        expand_updated.astype(jnp.bfloat16),
        shrink_average,
        shrink_variance,
        shrink_updated,
        shrink_updated.astype(jnp.bfloat16),
        gains_average,
        gains_variance,
        gains_updated,
    )


def solution(mesh):
    in_specs = (
        P("fsdp", "seq", None),
        P("fsdp", "seq", None),
        P("fsdp"),
        P("seq", "fsdp"),
        P("seq", "fsdp"),
        P("seq", "fsdp"),
        P("fsdp", "seq"),
        P(),
        P(None, "seq", None),
        P("fsdp", None),
        P("seq", "fsdp"),
        P("seq", "fsdp"),
        P("seq", "fsdp"),
        P("seq", "fsdp"),
        P("seq", "fsdp"),
        P("seq", "fsdp"),
        P("fsdp", "seq"),
        P("fsdp", "seq"),
        P(),
        P(),
    )
    out_specs = (
        P("fsdp", "seq", None),
        P("fsdp", "seq", None),
        P("seq", "fsdp"),
        P("seq", "fsdp"),
        P("seq", "fsdp"),
        P("fsdp", "seq"),
        P(),
        P("seq", "fsdp"),
        P("seq", "fsdp"),
        P("seq", "fsdp"),
        P("seq", "fsdp"),
        P("seq", "fsdp"),
        P("seq", "fsdp"),
        P("seq", "fsdp"),
        P("seq", "fsdp"),
        P("seq", "fsdp"),
        P("seq", "fsdp"),
        P("seq", "fsdp"),
        P("seq", "fsdp"),
        P("fsdp", "seq"),
        P("fsdp", "seq"),
        P("fsdp", "seq"),
        P("fsdp", "seq"),
        P(),
        P(),
        P(),
    )
    return jax.shard_map(body, mesh=mesh, in_specs=in_specs, out_specs=out_specs, check_vma=False)
```

profile of v0, /device:TPU:0, one launch (start us, length us, event | category | flops | bytes accessed | tf_op | source)
XLA Modules:
  0.0 3937.3 jit_solution(1679490623924742357)
XLA Ops:
  25.9 93.0 %all-gather.13.cloned.1.call-done = bf16[1024,3072]{1,0:T(8,128)(2,1)} async-done(((bf16[128,3072]{1,0:T(8,128)(2,1)}), bf16[1024,3072]{1,0:T(8,128)(2,1)}) %all-gather.13.cloned.1.call-update) | async-done | bytes 6291472 | tf_op jit(solution)/shard_map/all_gather | solution.py:155
  205.7 162.2 %all-gather.31.cloned.1.call-done = bf16[8192,1024]{1,0:T(8,128)(2,1)} async-done(((bf16[1024,1024]{1,0:T(8,128)(2,1)}), bf16[8192,1024]{1,0:T(8,128)(2,1)}) %all-gather.31.cloned.1.call-update) | async-done | bytes 16777232 | tf_op jit(solution)/shard_map/all_gather | solution.py:208
  367.9 21.7 copy.119
  389.6 206.7 %all-gather.29.cloned.1.call-done = bf16[8192,1024]{1,0:T(8,128)(2,1)} async-done(((bf16[1024,1024]{1,0:T(8,128)(2,1)}), bf16[8192,1024]{1,0:T(8,128)(2,1)}) %all-gather.29.cloned.1.call-update) | async-done | bytes 16777232 | tf_op jit(solution)/shard_map/all_gather | solution.py:207
  617.2 638.4 %while.30 = (s32[]{:T(128)}, f32[1,1024,16,64]{1,3,2,0:T(8,128)}, f32[1,1024,16]{1,2,0:T(8,128)S(1)}, f32[1,1024,16]{1,2,0:T(8,128)S(1)}, s32[8]{0:T(128)S(1)}, ...) while((s32[]{:T(128)}, f32[1,1024,16,64]{1,3,2,0:T(8,128)}, ...), condition=%wide.region_5.6_spmd.clone, body=%wide.region_2.5_spmd.clone.sunk | while | flops 4482762752 | bytes 225448144 | solution.py:103
  623.1 24.0 bitcast_reduce_fusion.2
  647.2 22.8 fusion.173
  670.0 26.8 bitcast_add_fusion.6
  702.7 25.2 bitcast_reduce_fusion.2
  728.0 21.8 fusion.173
  749.8 28.1 bitcast_add_fusion.6
  783.9 24.1 bitcast_reduce_fusion.2
  808.0 22.0 fusion.173
  830.0 28.6 bitcast_add_fusion.6
  864.7 24.0 bitcast_reduce_fusion.2
  910.2 27.9 bitcast_add_fusion.6
  944.1 23.9 bitcast_reduce_fusion.2
  989.4 27.9 bitcast_add_fusion.6
  1023.3 23.9 bitcast_reduce_fusion.2
  1068.7 27.9 bitcast_add_fusion.6
  1102.6 23.9 bitcast_reduce_fusion.2
  1148.0 27.9 bitcast_add_fusion.6
  1181.9 23.9 bitcast_reduce_fusion.2
  1227.3 27.9 bitcast_add_fusion.6
  1290.3 33.2 fusion.58
  1342.8 28.5 multiply_reduce_fusion
  1419.6 1077.7 %while.31 = (s32[]{:T(128)}, f32[1,1024,16,64]{1,3,2,0:T(8,128)}, bf16[1,8192,1024]{1,2,0:T(8,128)(2,1)}, bf16[1,8192,1024]{1,2,0:T(8,128)(2,1)}, s32[8]{0:T(128...) while((s32[]{:T(128)}, f32[1,1024,16,64]{1,3,2,0:T(8,128)}, ...), condition=%wide.region_12.13_spmd.clone, body=%wide.region_11.12_spmd.clone.sunk | while | flops 10907289600 | bytes 363007264 | solution.py:103
  1426.8 23.5 fusion.184
  1450.3 26.5 fusion.186
  1476.7 41.3 %fusion.185 = bf16[1024,16,1024]{0,2,1:T(8,128)(2,1)} fusion(f32[16,1024,1024]{2,1,0:T(8,128)} %fusion.184, f32[1024,16]{0,1:T(8,128)S(1)} %bitcast.428, f32[1024,16]{0,1:T(8,128)S(1)} %bitcast.430, pred[1024]{0:T(1024)(128)(4,1)S(1)} %add_compare_fusion.5, bf16[1024,16,64]{0,2,1:T(8,128)(2,1)} %bitcast.401, ...), kind=kOutput, calls=%fused_computation.31.clone.1 | convolution fusion | flops 2248146944 | bytes 104989696 | tf_op jit(solution)/shard_map/while/body/eval_jaxpr/rqhd,rkhd->rqhk/dot_general | solution.py:87
  1561.8 23.2 fusion.184
  1585.0 25.8 fusion.186
  1610.8 40.8 %fusion.185 = bf16[1024,16,1024]{0,2,1:T(8,128)(2,1)} fusion(f32[16,1024,1024]{2,1,0:T(8,128)} %fusion.184, f32[1024,16]{0,1:T(8,128)S(1)} %bitcast.428, f32[1024,16]{0,1:T(8,128)S(1)} %bitcast.430, pred[1024]{0:T(1024)(128)(4,1)S(1)} %add_compare_fusion.5, bf16[1024,16,64]{0,2,1:T(8,128)(2,1)} %bitcast.401, ...), kind=kOutput, calls=%fused_computation.31.clone.1 | convolution fusion | flops 2248146944 | bytes 104989696 | tf_op jit(solution)/shard_map/while/body/eval_jaxpr/rqhd,rkhd->rqhk/dot_general | solution.py:87
  1696.4 23.2 fusion.184
  1719.5 25.8 fusion.186
  1745.4 40.8 %fusion.185 = bf16[1024,16,1024]{0,2,1:T(8,128)(2,1)} fusion(f32[16,1024,1024]{2,1,0:T(8,128)} %fusion.184, f32[1024,16]{0,1:T(8,128)S(1)} %bitcast.428, f32[1024,16]{0,1:T(8,128)S(1)} %bitcast.430, pred[1024]{0:T(1024)(128)(4,1)S(1)} %add_compare_fusion.5, bf16[1024,16,64]{0,2,1:T(8,128)(2,1)} %bitcast.401, ...), kind=kOutput, calls=%fused_computation.31.clone.1 | convolution fusion | flops 2248146944 | bytes 104989696 | tf_op jit(solution)/shard_map/while/body/eval_jaxpr/rqhd,rkhd->rqhk/dot_general | solution.py:87
  1831.0 23.2 fusion.184
  1854.2 25.8 fusion.186
  1880.0 40.8 %fusion.185 = bf16[1024,16,1024]{0,2,1:T(8,128)(2,1)} fusion(f32[16,1024,1024]{2,1,0:T(8,128)} %fusion.184, f32[1024,16]{0,1:T(8,128)S(1)} %bitcast.428, f32[1024,16]{0,1:T(8,128)S(1)} %bitcast.430, pred[1024]{0:T(1024)(128)(4,1)S(1)} %add_compare_fusion.5, bf16[1024,16,64]{0,2,1:T(8,128)(2,1)} %bitcast.401, ...), kind=kOutput, calls=%fused_computation.31.clone.1 | convolution fusion | flops 2248146944 | bytes 104989696 | tf_op jit(solution)/shard_map/while/body/eval_jaxpr/rqhd,rkhd->rqhk/dot_general | solution.py:87
  1965.6 23.2 fusion.184
  1988.8 25.8 fusion.186
  2014.6 40.8 %fusion.185 = bf16[1024,16,1024]{0,2,1:T(8,128)(2,1)} fusion(f32[16,1024,1024]{2,1,0:T(8,128)} %fusion.184, f32[1024,16]{0,1:T(8,128)S(1)} %bitcast.428, f32[1024,16]{0,1:T(8,128)S(1)} %bitcast.430, pred[1024]{0:T(1024)(128)(4,1)S(1)} %add_compare_fusion.5, bf16[1024,16,64]{0,2,1:T(8,128)(2,1)} %bitcast.401, ...), kind=kOutput, calls=%fused_computation.31.clone.1 | convolution fusion | flops 2248146944 | bytes 104989696 | tf_op jit(solution)/shard_map/while/body/eval_jaxpr/rqhd,rkhd->rqhk/dot_general | solution.py:87
  2100.2 23.2 fusion.184
  2123.3 25.8 fusion.186
  2149.1 40.8 %fusion.185 = bf16[1024,16,1024]{0,2,1:T(8,128)(2,1)} fusion(f32[16,1024,1024]{2,1,0:T(8,128)} %fusion.184, f32[1024,16]{0,1:T(8,128)S(1)} %bitcast.428, f32[1024,16]{0,1:T(8,128)S(1)} %bitcast.430, pred[1024]{0:T(1024)(128)(4,1)S(1)} %add_compare_fusion.5, bf16[1024,16,64]{0,2,1:T(8,128)(2,1)} %bitcast.401, ...), kind=kOutput, calls=%fused_computation.31.clone.1 | convolution fusion | flops 2248146944 | bytes 104989696 | tf_op jit(solution)/shard_map/while/body/eval_jaxpr/rqhd,rkhd->rqhk/dot_general | solution.py:87
  2234.7 23.2 fusion.184
  2257.9 25.8 fusion.186
  2283.7 40.8 %fusion.185 = bf16[1024,16,1024]{0,2,1:T(8,128)(2,1)} fusion(f32[16,1024,1024]{2,1,0:T(8,128)} %fusion.184, f32[1024,16]{0,1:T(8,128)S(1)} %bitcast.428, f32[1024,16]{0,1:T(8,128)S(1)} %bitcast.430, pred[1024]{0:T(1024)(128)(4,1)S(1)} %add_compare_fusion.5, bf16[1024,16,64]{0,2,1:T(8,128)(2,1)} %bitcast.401, ...), kind=kOutput, calls=%fused_computation.31.clone.1 | convolution fusion | flops 2248146944 | bytes 104989696 | tf_op jit(solution)/shard_map/while/body/eval_jaxpr/rqhd,rkhd->rqhk/dot_general | solution.py:87
  2369.3 23.2 fusion.184
  2392.5 25.8 fusion.186
  2418.3 40.8 %fusion.185 = bf16[1024,16,1024]{0,2,1:T(8,128)(2,1)} fusion(f32[16,1024,1024]{2,1,0:T(8,128)} %fusion.184, f32[1024,16]{0,1:T(8,128)S(1)} %bitcast.428, f32[1024,16]{0,1:T(8,128)S(1)} %bitcast.430, pred[1024]{0:T(1024)(128)(4,1)S(1)} %add_compare_fusion.5, bf16[1024,16,64]{0,2,1:T(8,128)(2,1)} %bitcast.401, ...), kind=kOutput, calls=%fused_computation.31.clone.1 | convolution fusion | flops 2248146944 | bytes 104989696 | tf_op jit(solution)/shard_map/while/body/eval_jaxpr/rqhd,rkhd->rqhk/dot_general | solution.py:87
  2498.2 23.4 convolution_convert_fusion
  2524.7 254.0 %reduce-scatter.28.cloned.1.call-done = bf16[1,1024,1024]{1,2,0:T(8,128)(2,1)} async-done(((bf16[1,8192,1024]{1,2,0:T(8,128)(2,1)}), bf16[1,1024,1024]{1,2,0:T(8,128)(2,1)}) %reduce-scatter.28.cloned.1.call-update) | async-done | bytes 2097168 | tf_op jit(solution)/shard_map/reduce_scatter | solution.py:276
  2795.7 268.4 %reduce-scatter.30.cloned.1.call-done = bf16[1,1024,1024]{1,2,0:T(8,128)(2,1)} async-done(((bf16[1,8192,1024]{1,2,0:T(8,128)(2,1)}), bf16[1,1024,1024]{1,2,0:T(8,128)(2,1)}) %reduce-scatter.30.cloned.1.call-update) | async-done | bytes 2097168 | tf_op jit(solution)/shard_map/reduce_scatter | solution.py:279
  3076.5 172.3 %reduce-scatter.40.cloned.1.call-done = bf16[128,5248]{1,0:T(8,128)(2,1)} async-done(((bf16[1024,5248]{1,0:T(8,128)(2,1)}), bf16[128,5248]{1,0:T(8,128)(2,1)}) %reduce-scatter.40.cloned.1.call-update) | async-done | bytes 1343504 | tf_op jit(solution)/shard_map/reduce_scatter | solution.py:304
  3301.3 116.7 %reduce-scatter.32.cloned.1.call-done = bf16[128,3072]{1,0:T(8,128)(2,1)} async-done(((bf16[1024,3072]{1,0:T(8,128)(2,1)}), bf16[128,3072]{1,0:T(8,128)(2,1)}) %reduce-scatter.32.cloned.1.call-update) | async-done | bytes 786448 | tf_op jit(solution)/shard_map/reduce_scatter | solution.py:298
  3418.1 29.0 reduce-scatter.46.cloned.1.call-done
  3455.2 57.6 %reduce-scatter.52.cloned.1.call-done = bf16[128,256]{1,0:T(8,128)(2,1)} async-done(((bf16[1024,256]{1,0:T(8,128)(2,1)}), bf16[128,256]{1,0:T(8,128)(2,1)}) %reduce-scatter.52.cloned.1.call-update) | async-done | bytes 65552
  3515.1 65.9 %reduce-scatter.56.cloned.1.call-done = bf16[128,656]{1,0:T(8,128)(2,1)} async-done(((bf16[1024,656]{1,0:T(8,128)(2,1)}), bf16[128,656]{1,0:T(8,128)(2,1)}) %reduce-scatter.56.cloned.1.call-update) | async-done | bytes 167952
  3611.2 70.2 %reduce-scatter.54.cloned.1.call-done = bf16[128,1312]{1,0:T(8,128)(2,1)} async-done(((bf16[1024,1312]{1,0:T(8,128)(2,1)}), bf16[128,1312]{1,0:T(8,128)(2,1)}) %reduce-scatter.54.cloned.1.call-update) | async-done | bytes 335888
  3717.6 32.5 all_gather.59
  3760.9 59.6 %reduce-scatter.50.cloned.1.call-done = bf16[128,768]{1,0:T(8,128)(2,1)} async-done(((bf16[1024,768]{1,0:T(8,128)(2,1)}), bf16[128,768]{1,0:T(8,128)(2,1)}) %reduce-scatter.50.cloned.1.call-update) | async-done | bytes 196624
  3845.7 42.6 %psum.7 = f32[2,1024]{1,0:T(2,128)S(1)} all-reduce(f32[2,1024]{1,0:T(2,128)S(1)} %pad_maximum_fusion.7), channel_id=1, replica_groups=mesh['seq'=8,'fsdp'=4] {'seq','fsdp'}, use_global_device_ids=true, to_apply=%region_27.28 | all-reduce | flops 2048 | bytes 16384 | tf_op jit(solution)/shard_map/psum | solution.py:325
  3895.3 31.5 all-gather.23.cloned.1.call-done
  (444 shorter events, 937.8 us)
Async XLA Ops:
  7.2 111.7 %all-gather.13.cloned.1.call-start = ((), (), s32[]{:S(2)}) async-start(), calls=%async_computation.15 | async-start | bytes 7077888 | tf_op jit(solution)/shard_map/all_gather | solution.py:155
  18.8 163.6 %all-gather.17.cloned.1.call-start = ((), (), s32[]{:S(2)}) async-start(), calls=%async_computation.17 | async-start | bytes 1679360 | tf_op jit(solution)/shard_map/all_gather | solution.py:151
  20.8 347.2 %all-gather.31.cloned.1.call-start = ((), (), s32[]{:S(2)}) async-start(), calls=%async_computation.33 | async-start | bytes 18874368 | tf_op jit(solution)/shard_map/all_gather | solution.py:208
  23.7 104.4 %copy-start.3 = (bf16[1,1024,1024]{1,2,0:T(8,128)(2,1)}, bf16[1,1024,1024]{1,2,0:T(8,128)(2,1)S(1)}, u32[]{:S(2)}) copy-start(bf16[1,1024,1024]{1,2,0:T(8,128)(2,1)S(1)} %copy.112) | copy-start | bytes 6291460
  24.1 104.0 %copy-start.35 = (f32[1024]{0:T(1024)}, f32[1024]{0:T(1024)S(1)}, u32[]{:S(2)}) copy-start(f32[1024]{0:T(1024)S(1)} %broadcast_multiply_fusion.4) | copy-start | bytes 12292
  25.3 102.8 %copy-start.41 = (f32[1024]{0:T(1024)}, f32[1024]{0:T(1024)S(1)}, u32[]{:S(2)}) copy-start(f32[1024]{0:T(1024)S(1)} %fusion.96) | copy-start | bytes 12292
  25.9 102.2 %copy-start.44 = (f32[1,1024]{1,0:T(1,128)}, f32[1,1024]{1,0:T(1,128)S(1)}, u32[]{:S(2)}) copy-start(f32[1,1024]{1,0:T(1,128)S(1)} %get-tuple-element.449) | copy-start | bytes 12292
  134.4 461.9 %all-gather.29.cloned.1.call-start = ((), (), s32[]{:S(2)}) async-start(), calls=%async_computation.32 | async-start | bytes 18874368 | tf_op jit(solution)/shard_map/all_gather | solution.py:207
  165.4 10.5 copy-start.33
  175.8 17.3 copy-start.24
  175.8 1084.8 %all-gather.15.cloned.1.call-start = ((), (), s32[]{:S(2)}) async-start(), calls=%async_computation.16 | async-start | bytes 2359296 | tf_op jit(solution)/shard_map/all_gather | solution.py:156
  182.3 1086.9 %all-gather.19.cloned.1.call-start = ((), (), s32[]{:S(2)}) async-start(), calls=%async_computation.18 | async-start | bytes 12091392 | tf_op jit(solution)/shard_map/all_gather | solution.py:157
  182.9 1107.4 %all-gather.21.cloned.1.call-start = ((), (), s32[]{:S(2)}) async-start(), calls=%async_computation.19 | async-start | bytes 6045696 | tf_op jit(solution)/shard_map/all_gather | solution.py:158
  191.5 2330.1 %reduce-scatter.36.cloned.1.call-start = ((), (), s32[]{:S(2)}) async-start(), calls=%async_computation.24 | async-start | bytes 2359296 | tf_op jit(solution)/shard_map/reduce_scatter | solution.py:301
  1255.7 10.4 copy-start
  1255.7 10.4 copy-start.15
  1266.2 105.1 %copy-start.50 = (f32[1024]{0:T(1024)}, f32[1024]{0:T(1024)S(1)}, u32[]{:S(2)}) copy-start(f32[1024]{0:T(1024)S(1)} %broadcast_multiply_fusion.3) | copy-start | bytes 12292
  1269.2 102.1 %copy-start.57 = (f32[1024]{0:T(1024)}, f32[1024]{0:T(1024)S(1)}, u32[]{:S(2)}) copy-start(f32[1024]{0:T(1024)S(1)} %fusion.97) | copy-start | bytes 12292
  1269.2 21.1 copy-start.9
  1269.2 21.1 copy-start.37
  1342.8 28.5 copy-start.53
  1383.1 1139.3 %reduce-scatter.48.cloned.1.call-start = ((), (), s32[]{:S(2)}) async-start(), calls=%async_computation.35 | async-start | bytes 6193152
  1407.5 1371.1 %reduce-scatter.28.cloned.1.call-start = ((), (), s32[]{:S(2)}) async-start(), calls=%async_computation.20 | async-start | bytes 18874368 | tf_op jit(solution)/shard_map/reduce_scatter | solution.py:276
  1536.5 15.9 copy-start.5
  1671.3 15.7 copy-start.5
  1805.9 15.7 copy-start.5
  1940.5 15.7 copy-start.5
  2075.2 15.7 copy-start.5
  2209.7 15.7 copy-start.5
  2344.3 15.7 copy-start.5
  2478.8 15.7 copy-start.5
  2497.4 566.8 %reduce-scatter.30.cloned.1.call-start = ((), (), s32[]{:S(2)}) async-start(), calls=%async_computation.21 | async-start | bytes 18874368 | tf_op jit(solution)/shard_map/reduce_scatter | solution.py:279
  2498.1 750.7 %reduce-scatter.40.cloned.1.call-start = ((), (), s32[]{:S(2)}) async-start(), calls=%async_computation.26 | async-start | bytes 12091392 | tf_op jit(solution)/shard_map/reduce_scatter | solution.py:304
  2521.5 257.1 %copy-start.31 = (f32[1024,64]{0,1:T(8,128)S(1)}, f32[1024,64]{0,1:T(8,128)}, u32[]{:S(2)}) copy-start(f32[1024,64]{0,1:T(8,128)} %get-tuple-element.446) | copy-start | bytes 786436
  2521.6 748.9 %reduce-scatter.38.cloned.1.call-start = ((), (), s32[]{:S(2)}) async-start(), calls=%async_computation.25 | async-start | bytes 327680 | tf_op jit(solution)/shard_map/reduce_scatter | solution.py:315
  2522.3 773.9 %reduce-scatter.42.cloned.1.call-start = ((), (), s32[]{:S(2)}) async-start(), calls=%async_computation.27 | async-start | bytes 839680 | tf_op jit(solution)/shard_map/reduce_scatter | solution.py:321
  2524.6 893.4 %reduce-scatter.32.cloned.1.call-start = ((), (), s32[]{:S(2)}) async-start(), calls=%async_computation.22 | async-start | bytes 7077888 | tf_op jit(solution)/shard_map/reduce_scatter | solution.py:298
  2789.3 274.8 %copy-start.4 = (bf16[1,1024,1024]{1,2,0:T(8,128)(2,1)S(1)}, bf16[1,1024,1024]{1,2,0:T(8,128)(2,1)}, u32[]{:S(2)}) copy-start(bf16[1,1024,1024]{1,2,0:T(8,128)(2,1)} %copy-done.3) | copy-start | bytes 6291460
  2789.3 274.8 %copy-start.36 = (f32[1024]{0:T(1024)S(1)}, f32[1024]{0:T(1024)}, u32[]{:S(2)}) copy-start(f32[1024]{0:T(1024)} %copy-done.35) | copy-start | bytes 12292
  2789.3 274.8 %copy-start.42 = (f32[1024]{0:T(1024)S(1)}, f32[1024]{0:T(1024)}, u32[]{:S(2)}) copy-start(f32[1024]{0:T(1024)} %copy-done.41) | copy-start | bytes 12292
  2789.3 274.8 %copy-start.45 = (f32[1,1024]{1,0:T(1,128)S(1)}, f32[1,1024]{1,0:T(1,128)}, u32[]{:S(2)}) copy-start(f32[1,1024]{1,0:T(1,128)} %copy-done.44) | copy-start | bytes 12292
  3076.5 370.6 %reduce-scatter.46.cloned.1.call-start = ((), (), s32[]{:S(2)}) async-start(), calls=%async_computation.34 | async-start | bytes 1679360
  3251.3 261.4 %reduce-scatter.52.cloned.1.call-start = ((), (), s32[]{:S(2)}) async-start(), calls=%async_computation.37 | async-start | bytes 589824
  3274.5 306.5 %reduce-scatter.56.cloned.1.call-start = ((), (), s32[]{:S(2)}) async-start(), calls=%async_computation.39 | async-start | bytes 1769472
  3301.2 304.5 %reduce-scatter.34.cloned.1.call-start = ((), (), s32[]{:S(2)}) async-start(), calls=%async_computation.23 | async-start | bytes 983040 | tf_op jit(solution)/shard_map/reduce_scatter | solution.py:312
  3418.0 263.3 %reduce-scatter.54.cloned.1.call-start = ((), (), s32[]{:S(2)}) async-start(), calls=%async_computation.38 | async-start | bytes 3244032
  3454.9 253.6 %reduce-scatter.44.cloned.1.call-start = ((), (), s32[]{:S(2)}) async-start(), calls=%async_computation.29 | async-start | bytes 327680 | tf_op jit(solution)/shard_map/reduce_scatter | solution.py:355
  3515.0 241.1 %all-gather.27.cloned.1.call-start = ((), (), s32[]{:S(2)}) async-start(), calls=%async_computation.31 | async-start | bytes 1511424 | tf_op jit(solution)/shard_map/all_gather | solution.py:382
  3584.1 236.3 %reduce-scatter.50.cloned.1.call-start = ((), (), s32[]{:S(2)}) async-start(), calls=%async_computation.36 | async-start | bytes 1769472
  3608.4 79.3 %copy-start.25 = (f32[128,768]{1,0:T(8,128)S(1)}, f32[128,768]{1,0:T(8,128)}, u32[]{:S(2)}) copy-start(f32[128,768]{1,0:T(8,128)} %param.27) | copy-start | bytes 1179652
  3611.1 81.4 %copy-start.38 = (f32[1024]{0:T(1024)S(1)}, f32[1024]{0:T(1024)}, u32[]{:S(2)}) copy-start(f32[1024]{0:T(1024)} %fusion.95) | copy-start | bytes 12292
  3611.1 277.9 %all-gather.25.cloned.1.call-start = ((), (), s32[]{:S(2)}) async-start(), calls=%async_computation.30 | async-start | bytes 3022848 | tf_op jit(solution)/shard_map/all_gather | solution.py:381
  3686.0 240.8 %all-gather.23.cloned.1.call-start = ((), (), s32[]{:S(2)}) async-start(), calls=%async_computation.28 | async-start | bytes 1769472 | tf_op jit(solution)/shard_map/all_gather | solution.py:379
  3703.9 52.2 %copy-start.29 = (f32[656,128]{1,0:T(8,128)S(1)}, f32[656,128]{1,0:T(8,128)}, u32[]{:S(2)}) copy-start(f32[656,128]{1,0:T(8,128)} %param.30) | copy-start | bytes 1007620
  3752.7 71.8 %copy-start.46 = (f32[1,1024]{1,0:T(1,128)S(1)}, f32[1,1024]{1,0:T(1,128)}, u32[]{:S(2)}) copy-start(f32[1,1024]{1,0:T(1,128)} %copy-done.44) | copy-start | bytes 12292
  3824.5 10.8 copy-start.49
  3824.5 10.9 copy-start.43
  3824.5 10.9 copy-start.47
  3841.6 46.7 %copy-start.55 = (f32[2,1024]{1,0:T(2,128)S(1)}, f32[2,1024]{1,0:T(2,128)}, u32[]{:S(2)}) copy-start(f32[2,1024]{1,0:T(2,128)} %param.31) | copy-start | bytes 24580
  3841.6 46.7 %copy-start.62 = (f32[2,1024]{1,0:T(2,128)S(1)}, f32[2,1024]{1,0:T(2,128)}, u32[]{:S(2)}) copy-start(f32[2,1024]{1,0:T(2,128)} %param.43) | copy-start | bytes 24580
  3841.6 46.7 %copy-start.63 = (f32[2,1024]{1,0:T(2,128)S(1)}, f32[2,1024]{1,0:T(2,128)}, u32[]{:S(2)}) copy-start(f32[2,1024]{1,0:T(2,128)} %param.42) | copy-start | bytes 24580
  3841.6 47.3 %copy-start.17 = (f32[128,1312]{0,1:T(8,128)S(1)}, f32[128,1312]{0,1:T(8,128)}, u32[]{:S(2)}) copy-start(f32[128,1312]{0,1:T(8,128)} %param.29) | copy-start | bytes 2015236
  3845.6 47.0 %copy-start.32 = (bf16[128,768]{1,0:T(8,128)(2,1)S(1)}, bf16[128,768]{1,0:T(8,128)(2,1)}, u32[]{:S(2)}) copy-start(bf16[128,768]{1,0:T(8,128)(2,1)} %reduce-scatter.34.cloned.1.call-done) | copy-start | bytes 589828
  3888.9 37.9 copy-start.26
  (40 other events, 161.4 us)
Sparse Core Ops, SparseCore 0:
  18.9 99.8 all-gather.12
  121.0 16.5 all-gather.16
  140.3 227.5 all-gather.30
  370.5 225.7 all-gather.28
  598.3 47.4 all-gather.14
  647.7 152.6 all-gather.18
  802.4 86.9 all-gather.20
  1383.2 66.1 reduce-scatter.35
  1453.0 105.3 reduce-scatter.47
  2497.5 281.1 reduce-scatter.27
  2782.5 281.6 reduce-scatter.29
  3068.0 180.7 reduce-scatter.39
  3251.3 19.1 reduce-scatter.37
  3273.6 22.5 reduce-scatter.41
  3300.0 117.9 reduce-scatter.31
  3421.1 25.9 reduce-scatter.45
  3450.9 61.8 reduce-scatter.51
  3517.0 63.8 reduce-scatter.55
  3583.5 22.2 reduce-scatter.33
  3609.6 71.7 reduce-scatter.53
  3684.5 19.2 reduce-scatter.43
  3706.4 47.2 all-gather.26
  3757.1 63.3 reduce-scatter.49
  3823.1 57.0 all-gather.24
  3883.1 43.6 all-gather.22
where the time goes:
time: 3950 us; the launch traced here: 3940 us
  waiting for transfers between devices  1650 us (42%)
  matrix products  1620 us (41%)
  other arithmetic  277 us (7%)
  local copies, waits for them, and re-layouts  258 us (7%)
  blocking collectives  106 us (3%)
    dot_general x16, matrix products, masked_scores(): jnp.einsum('rqhd,rkhd->rqhk', query_part, key_part, preferred_element_typ...  379 us
    dot_general x8, matrix products, shared_terms(): jnp.einsum('rqhd,rkhd->rqhk', back_part, value_part, preferred_element_ty...  327 us
    unnamed x31, waiting for transfers between devices  284 us
    reduce_scatter x1, waiting for transfers between devices, body(): lax.psum_scatter(back_result[2].astype(jnp.bfloat16), 'seq', scatter_dime...  268 us
    reduce_scatter x1, waiting for transfers between devices, body(): lax.psum_scatter(back_result[1].astype(jnp.bfloat16), 'seq', scatter_dime...  254 us
    dot_general x8, matrix products, forward_piece(): jnp.einsum('rqhk,rkhd->rqhd', weights.astype(jnp.bfloat16), value_part, p...  223 us
    dot_general x8, matrix products, summed_piece(): jnp.einsum('rqhk,rqhd->rkhd', chance_low, attend_heads, preferred_element...  207 us
    all_gather x1, waiting for transfers between devices, body(): lax.all_gather(flat_keys, 'seq', axis=1, tiled=True)  207 us
  transfers between devices with their start and end apart: 25, of which 16 were waited for; matrix products, arithmetic and copies ran while one was open for 52% of the time, Pallas kernels for 0%

commit v1 on v0

v1 whole, which is shorter than its diff:
```python
import functools
import math

import jax
import jax.numpy as jnp
from jax import lax
from jax.experimental import pallas as pl
from jax.experimental.pallas import tpu as pltpu
from jax.sharding import Mesh
from jax.sharding import PartitionSpec as P

HEADS = 16
HEAD_DIM = 64
FF = 2624
STEP = 10


ROPE_BASE = 160000.0
NORM_EPS = 1e-05
NEG_LARGE = -1e30
BETA_ONE = 0.95
BETA_TWO = 0.95
ADAM_EPS = 1e-08
DECAY_RATE = 0.01
WEIGHT_RATES = (0.03, 1.0, 0.03, 0.03)
GAINS_RATE = 0.8


def layer_norm(values, gain):
    centre = values - jnp.mean(values, axis=-1, keepdims=True)
    spread = jnp.mean(centre * centre, axis=-1, keepdims=True)
    return centre * lax.rsqrt(spread + NORM_EPS) * gain


def rotary_tables(position):
    halves = HEAD_DIM // 2
    frequency = ROPE_BASE ** (-2.0 * jnp.arange(halves, dtype=jnp.float32) / HEAD_DIM)
    angle = frequency[:, None] * position.astype(jnp.float32)[None, :]
    return jnp.cos(angle), jnp.sin(angle)


def outer_sum(left, right):
    return lax.dot_general(
        left, right, (((0,), (0,)), ((), ())), preferred_element_type=jnp.float32
    )


def back_product(left, right):
    return lax.dot_general(
        left, right, (((1,), (1,)), ((), ())), preferred_element_type=jnp.float32
    )


def plain_product(left, right):
    return jnp.dot(left, right, preferred_element_type=jnp.float32)


NT = (((1,), (1,)), ((), ()))
SAFE_BOUND = 60.0
MASK = -1e30
VMEM_LIMIT = 60 * 1024 * 1024


def extra_rows(rows, length, size=HEAD_DIM):
    place = lax.broadcasted_iota(jnp.int32, (size, length), 0)
    block = jnp.zeros((size, length), jnp.float32)
    for index, row in enumerate(rows):
        block = jnp.where(place == index, row, block)
    return block.astype(jnp.bfloat16)


def three_parts(row):
    high = row.astype(jnp.bfloat16).astype(jnp.float32)
    middle = (row - high).astype(jnp.bfloat16).astype(jnp.float32)
    return [high, middle, row - high - middle]


def mask_row(start, length, limit):
    place = start + lax.broadcasted_iota(jnp.int32, (1, length), 1)
    return jnp.where(place < limit, 0.0, MASK)


def project_kernel(pieces_ref, first_ref, cosine_ref, sine_ref, out_ref, rows_ref):
    shards, _, heads = pieces_ref.shape[:3]
    lanes = pieces_ref.shape[-1]
    weight = jnp.concatenate(
        [pieces_ref[shard].reshape(3 * heads * HEAD_DIM, lanes) for shard in range(shards)], axis=1
    )
    product = lax.dot_general(weight, first_ref[...], NT, preferred_element_type=jnp.float32)
    cosine, sine = cosine_ref[...], sine_ref[...]
    half = HEAD_DIM // 2
    for head in range(heads):
        for part in range(3):
            base = (part * heads + head) * HEAD_DIM
            rows_ref[head, part] = weight[base : base + HEAD_DIM]
        for part, scale in ((0, HEAD_DIM**-0.5), (1, 1.0)):
            base = (part * heads + head) * HEAD_DIM
            upper, lower = product[base : base + half], product[base + half : base + HEAD_DIM]
            turned_upper = (upper * cosine - lower * sine).astype(jnp.bfloat16)
            turned_lower = (lower * cosine + upper * sine).astype(jnp.bfloat16)
            place = part * HEAD_DIM
            out_ref[head, place : place + half, :] = turned_upper * jnp.bfloat16(scale)
            out_ref[head, place + half : place + HEAD_DIM, :] = turned_lower * jnp.bfloat16(
                scale
            )
        base = (2 * heads + head) * HEAD_DIM
        out_ref[head, 2 * HEAD_DIM :, :] = product[base : base + HEAD_DIM].astype(jnp.bfloat16)


def project_heads(pieces, first, cosine, sine, phases, phase):
    shards, lanes = pieces.shape[0], pieces.shape[-1]
    count, width = first.shape
    pieces = pieces.reshape(shards, 3, shards, phases, HEAD_DIM, lanes)
    group = min(4, shards)
    half = HEAD_DIM // 2
    return pl.pallas_call(
        project_kernel,
        grid=(shards // group,),
        in_specs=[
            pl.BlockSpec(
                (shards, 3, group, None, HEAD_DIM, lanes), lambda g: (0, 0, g, phase, 0, 0)
            ),
            pl.BlockSpec((count, width), lambda g: (0, 0)),
            pl.BlockSpec((half, count), lambda g: (0, 0)),
            pl.BlockSpec((half, count), lambda g: (0, 0)),
        ],
        out_specs=[
            pl.BlockSpec((group, 3 * HEAD_DIM, count), lambda g: (g, 0, 0)),
            pl.BlockSpec((group, 3, HEAD_DIM, width), lambda g: (g, 0, 0, 0)),
        ],
        out_shape=[
            jax.ShapeDtypeStruct((shards, 3 * HEAD_DIM, count), jnp.bfloat16),
            jax.ShapeDtypeStruct((shards, 3, HEAD_DIM, width), jnp.bfloat16),
        ],
        compiler_params=pltpu.CompilerParams(vmem_limit_bytes=VMEM_LIMIT),
        cost_estimate=pl.CostEstimate(
            flops=6 * width * width * count // phases,
            bytes_accessed=20 * width * width // phases,
            transcendentals=0,
        ),
    )(pieces, first, cosine, sine)


def forward_kernel(
    length_ref,
    own_ref,
    other_ref,
    out_ref,
    log_ref,
    query_ref,
    key_ref,
    value_ref,
    peak_ref,
    bound_ref,
):
    row, index = pl.program_id(0), pl.program_id(1)
    shards, _, local = own_ref.shape
    limit = length_ref[row]
    ratio = max(1, 2048 // local)
    blocks = (limit + local - 1) // local

    def prepare(joint_ref, first):
        query_most = jnp.zeros((1, 1), jnp.float32)
        key_most = jnp.zeros((1, 1), jnp.float32)
        for shard in range(shards):
            place = slice(shard * local, (shard + 1) * local)
            key = joint_ref[shard, HEAD_DIM : 2 * HEAD_DIM, :]
            wide_key = key.astype(jnp.float32)
            key_size = jnp.sum(wide_key * wide_key, axis=0, keepdims=True)
            key_most = jnp.maximum(key_most, jnp.max(key_size, axis=1, keepdims=True))
            extra = extra_rows([mask_row(shard * local, local, limit), 1.0], local)
            key_ref[place, :] = jnp.concatenate([key, extra], axis=0).T
            value_ref[:HEAD_DIM, place] = joint_ref[shard, 2 * HEAD_DIM :, :]
            value_ref[HEAD_DIM:, place] = extra_rows([1.0], local, 16)
        for block in range(shards // 2):
            query = joint_ref[2 * block + first, :HEAD_DIM, :]
            wide_query = query.astype(jnp.float32)
            query_size = jnp.sum(wide_query * wide_query, axis=0, keepdims=True)
            query_most = jnp.maximum(query_most, jnp.max(query_size, axis=1, keepdims=True))
            query_ref[block] = query
        bound_ref[0] = (jnp.sqrt(query_most) * jnp.sqrt(key_most))[0, 0]

    for which, joint_ref in enumerate((own_ref, other_ref)):
        pl.when((index == 0) & (row == which))(
            functools.partial(prepare, joint_ref, which)
        )

    mine = 2 * index + row < blocks

    @pl.when(jnp.logical_not(mine))
    def padding():
        out_ref[...] = jnp.zeros_like(out_ref)
        log_ref[...] = jnp.zeros_like(log_ref)

    @pl.when(mine)
    def compute():
        query = query_ref[index]
        peak_ref[...] = jnp.zeros_like(peak_ref)

        @pl.when(bound_ref[0] > SAFE_BOUND)
        def find_peak():
            plain = jnp.concatenate([query, extra_rows([1.0], local)], axis=0)

            def step(block, peak):
                place = pl.ds(pl.multiple_of(block * local, local), local)
                scores = jnp.dot(key_ref[place, :], plain, preferred_element_type=jnp.float32)
                return jnp.maximum(peak, jnp.max(scores, axis=0, keepdims=True))

            peak = lax.fori_loop(0, blocks, step, jnp.full((1, local), MASK, jnp.float32))
            peak_ref[...] = peak.astype(jnp.bfloat16).astype(jnp.float32)

        peak = peak_ref[...]
        augmented = jnp.concatenate([query, extra_rows([1.0, -peak], local)], axis=0)

        def attend(start, size, total):
            place = pl.ds(pl.multiple_of(start, local), size)
            scores = jnp.dot(key_ref[place, :], augmented, preferred_element_type=jnp.float32)
            weights = jnp.exp(scores).astype(jnp.bfloat16)
            return total + jnp.dot(
                value_ref[:, place], weights, preferred_element_type=jnp.float32
            )

        large = blocks // ratio
        total = lax.fori_loop(
            0,
            large,
            lambda block, total: attend(block * (ratio * local), ratio * local, total),
            jnp.zeros((HEAD_DIM + 16, local), jnp.float32),
        )
        total = lax.fori_loop(
            large * ratio, blocks, lambda block, total: attend(block * local, local, total), total
        )
        mass = total[HEAD_DIM : HEAD_DIM + 1, :]
        out_ref[0, 0] = (total[:HEAD_DIM, :] / mass).astype(jnp.bfloat16)
        log_ref[0, 0] = peak + jnp.log(mass)


def attend_forward(lengths, own, other):
    shards, _, local = own.shape
    total = shards * local
    half = shards // 2
    joint = pl.BlockSpec((shards, 3 * HEAD_DIM, local), lambda r, i: (0, 0, 0))
    return pl.pallas_call(
        forward_kernel,
        grid=(2, half),
        in_specs=[pl.BlockSpec(memory_space=pltpu.SMEM), joint, joint],
        out_specs=[
            pl.BlockSpec((1, 1, HEAD_DIM, local), lambda r, i: (r, i, 0, 0)),
            pl.BlockSpec((1, 1, 1, local), lambda r, i: (r, i, 0, 0)),
        ],
        out_shape=[
            jax.ShapeDtypeStruct((2, half, HEAD_DIM, local), jnp.bfloat16),
            jax.ShapeDtypeStruct((2, half, 1, local), jnp.float32),
        ],
        scratch_shapes=[
            pltpu.VMEM((half, HEAD_DIM, local), jnp.bfloat16),
            pltpu.VMEM((total, 2 * HEAD_DIM), jnp.bfloat16),
            pltpu.VMEM((HEAD_DIM + 16, total), jnp.bfloat16),
            pltpu.VMEM((1, local), jnp.float32),
            pltpu.SMEM((1,), jnp.float32),
        ],
        compiler_params=pltpu.CompilerParams(vmem_limit_bytes=VMEM_LIMIT),
        cost_estimate=pl.CostEstimate(
            flops=10 * HEAD_DIM * total * total,
            bytes_accessed=16 * HEAD_DIM * total,
            transcendentals=total * total,
        ),
    )(lengths, own, other)


def backward_kernel(
    length_ref,
    own_ref,
    other_ref,
    own_back_ref,
    other_back_ref,
    out_ref,
    log_ref,
    cosine_ref,
    sine_ref,
    own_grad_ref,
    other_grad_ref,
    query_ref,
    wide_ref,
    query_flat,
    back_flat,
    query_sum,
):
    row, index = pl.program_id(0), pl.program_id(1)
    shards, _, local = own_ref.shape
    limit = length_ref[row]
    ratio = max(1, 2048 // local)
    blocks = (limit + local - 1) // local
    mine = (blocks + 1 - row) // 2
    half = HEAD_DIM // 2

    def turned_back(wide, shard):
        cosine, sine = cosine_ref[shard], sine_ref[shard]
        upper, lower = wide[:half], wide[half:]
        return jnp.concatenate(
            [upper * cosine + lower * sine, lower * cosine - upper * sine], axis=0
        ).astype(jnp.bfloat16)

    def prepare(joint_ref, back_ref, first):
        for block in range(shards // 2):
            place = slice(block * local, (block + 1) * local)
            query = joint_ref[2 * block + first, :HEAD_DIM, :]
            back = back_ref[2 * block + first]
            extra = extra_rows([1.0] + three_parts(-log_ref[first, block]), local)
            query_ref[place, :] = jnp.concatenate([query, extra], axis=0).T
            balance = jnp.sum(
                back.astype(jnp.float32) * out_ref[first, block].astype(jnp.float32),
                axis=0,
                keepdims=True,
            )
            extra = extra_rows(three_parts(-balance), local)
            wide_ref[place, :] = jnp.concatenate([back, extra], axis=0).T
            query_flat[:, place] = query
            back_flat[:, place] = back
        query_sum[...] = jnp.zeros_like(query_sum)

    def work(joint_ref, grad_ref):
        key = joint_ref[index, HEAD_DIM : 2 * HEAD_DIM, :]
        value = joint_ref[index, 2 * HEAD_DIM :, :]
        mask = mask_row(index * local, local, limit)
        wide_key = jnp.concatenate([key, extra_rows([mask, 1.0, 1.0, 1.0], local)], axis=0)
        wide_value = jnp.concatenate([value, extra_rows([1.0, 1.0, 1.0], local)], axis=0)

        def gather(start, size, carry):
            key_sum, value_sum = carry
            place = pl.ds(pl.multiple_of(start, local), size)
            scores = jnp.dot(query_ref[place, :], wide_key, preferred_element_type=jnp.float32)
            chance = jnp.exp(scores)
            change = jnp.dot(wide_ref[place, :], wide_value, preferred_element_type=jnp.float32)
            chance_low = chance.astype(jnp.bfloat16)
            score_back = (chance * change).astype(jnp.bfloat16)
            value_sum = value_sum + jnp.dot(
                back_flat[:, place], chance_low, preferred_element_type=jnp.float32
            )
            key_sum = key_sum + jnp.dot(
                query_flat[:, place], score_back, preferred_element_type=jnp.float32
            )
            query_sum[:, place] += lax.dot_general(
                key, score_back, NT, preferred_element_type=jnp.float32
            )
            return (key_sum, value_sum)

        large = mine // ratio
        zero = jnp.zeros((HEAD_DIM, local), jnp.float32)
        carry = lax.fori_loop(
            0,
            large,
            lambda block, carry: gather(block * (ratio * local), ratio * local, carry),
            (zero, zero),
        )
        key_sum, value_sum = lax.fori_loop(
            large * ratio, mine, lambda block, carry: gather(block * local, local, carry), carry
        )
        grad_ref[index, HEAD_DIM : 2 * HEAD_DIM, :] = turned_back(key_sum, index)
        grad_ref[index, 2 * HEAD_DIM :, :] = value_sum.astype(jnp.bfloat16)

    def padding(grad_ref):
        grad_ref[index, HEAD_DIM:, :] = jnp.zeros((2 * HEAD_DIM, local), jnp.bfloat16)

    def finish(grad_ref, first):
        for block in range(shards // 2):
            place = slice(block * local, (block + 1) * local)
            shard = 2 * block + first
            grad_ref[shard, :HEAD_DIM, :] = turned_back(
                query_sum[:, place] * HEAD_DIM**-0.5, shard
            )
            grad_ref[shard + 1 - 2 * first, :HEAD_DIM, :] = jnp.zeros(
                (HEAD_DIM, local), jnp.bfloat16
            )

    sides = ((own_ref, own_back_ref, own_grad_ref), (other_ref, other_back_ref, other_grad_ref))
    for which, (joint_ref, back_ref, grad_ref) in enumerate(sides):
        here = row == which
        pl.when(here & (index == 0))(functools.partial(prepare, joint_ref, back_ref, which))
        pl.when(here & (index < blocks))(functools.partial(work, joint_ref, grad_ref))
        pl.when(here & (index >= blocks))(functools.partial(padding, grad_ref))
        pl.when(here & (index == shards - 1))(functools.partial(finish, grad_ref, which))


def attend_backward(lengths, own, other, own_back, other_back, out, log_mass, cosine, sine):
    shards, _, local = own.shape
    total = shards * local
    half = shards // 2
    whole = lambda *shape: pl.BlockSpec(shape, lambda r, i: (0,) * len(shape))
    grad = jax.ShapeDtypeStruct((shards, 3 * HEAD_DIM, local), jnp.bfloat16)
    return pl.pallas_call(
        backward_kernel,
        grid=(2, shards),
        in_specs=[pl.BlockSpec(memory_space=pltpu.SMEM)]
        + [whole(shards, 3 * HEAD_DIM, local)] * 2
        + [whole(shards, HEAD_DIM, local)] * 2
        + [whole(2, half, HEAD_DIM, local), whole(2, half, 1, local)]
        + [whole(shards, HEAD_DIM // 2, local)] * 2,
        out_specs=[whole(shards, 3 * HEAD_DIM, local)] * 2,
        out_shape=[grad, grad],
        scratch_shapes=[
            pltpu.VMEM((total // 2, 2 * HEAD_DIM), jnp.bfloat16),
            pltpu.VMEM((total // 2, 2 * HEAD_DIM), jnp.bfloat16),
            pltpu.VMEM((HEAD_DIM, total // 2), jnp.bfloat16),
            pltpu.VMEM((HEAD_DIM, total // 2), jnp.bfloat16),
            pltpu.VMEM((HEAD_DIM, total // 2), jnp.float32),
        ],
        compiler_params=pltpu.CompilerParams(vmem_limit_bytes=VMEM_LIMIT),
        cost_estimate=pl.CostEstimate(
            flops=26 * HEAD_DIM * total * total,
            bytes_accessed=40 * HEAD_DIM * total,
            transcendentals=total * total,
        ),
    )(lengths, own, other, own_back, other_back, out, log_mass, cosine, sine)


TN = (((0,), (0,)), ((), ()))
PLAIN = (((1,), (0,)), ((), ()))
LANES = 128
GROUPS = 4
RUNS = 8
UNITS = FF // GROUPS
EXPAND_RUN = -(-2 * UNITS // (16 * RUNS)) * 16
SHRINK_RUN = -(-UNITS // (16 * RUNS)) * 16


def run_segments(start, stop, run):
    segments = []
    while start < stop:
        index = start // run
        end = min(stop, (index + 1) * run)
        segments.append((index, start - index * run, start, end - start))
        start = end
    return segments


def feed_kernel(
    second_ref,
    upstream_ref,
    active_ref,
    gate_ref,
    shrink_ref,
    shrunk_ref,
    second_back_ref,
    parts_ref,
    grads_ref,
    zero_ref,
    send_ref,
    zero_send_ref,
):
    index = pl.program_id(0)

    def joined(ref):
        return jnp.concatenate([ref[piece, 0] for piece in range(ref.shape[0])], axis=1)

    def product(left, right, dims):
        return lax.dot_general(left, right, dims, preferred_element_type=jnp.float32)

    def grad_copies(half, pair):
        moves = []
        for kind, member in ((0, pair), (1, pair + 2)):
            for run, place, offset, size in run_segments(
                half * UNITS, (half + 1) * UNITS, EXPAND_RUN
            ):
                moves.append((kind, offset - half * UNITS, run, member, place, size))
        for run, place, offset, size in run_segments(0, UNITS, SHRINK_RUN):
            moves.append((2, offset, run, 2 * pair + half, EXPAND_RUN + place, size))
        return [
            pltpu.make_async_copy(
                grads_ref.at[half, kind, pl.ds(offset, size), :],
                parts_ref.at[run, member, pl.ds(place, size), :],
                send_ref.at[half, number],
            )
            for number, (kind, offset, run, member, place, size) in enumerate(moves)
        ]

    def zero_copies():
        moves = []
        for member in range(GROUPS):
            for base, run_size, total in ((0, EXPAND_RUN, 2 * UNITS), (EXPAND_RUN, SHRINK_RUN, UNITS)):
                for run, place, _, size in run_segments(total, RUNS * run_size, run_size):
                    moves.append((run, member, base + place, size))
        return [
            pltpu.make_async_copy(
                zero_ref.at[pl.ds(0, size), :],
                parts_ref.at[run, member, pl.ds(place, size), :],
                zero_send_ref.at[number],
            )
            for number, (run, member, place, size) in enumerate(moves)
        ]

    @pl.when(index == 0)
    def fill():
        zero_ref[...] = jnp.zeros_like(zero_ref)
        for copy in zero_copies():
            copy.start()

    active, gate, shrink = joined(active_ref), joined(gate_ref), joined(shrink_ref)
    second, upstream = second_ref[...], upstream_ref[...]
    input_active = product(second, active, NT)
    input_gate = product(second, gate, NT)
    hidden_back = product(upstream, shrink, NT)
    below = 0.5 + 0.5 * lax.erf(input_active * 0.5**0.5)
    bell = jnp.exp(-0.5 * input_active * input_active) * (0.5 / math.pi) ** 0.5
    curve = input_active * below
    hidden = (curve * input_gate).astype(jnp.bfloat16)
    active_back = (hidden_back * input_gate * (below + input_active * bell)).astype(jnp.bfloat16)
    gate_back = (hidden_back * curve).astype(jnp.bfloat16)
    shrunk = product(hidden, shrink, PLAIN)
    second_back = product(active_back, active, PLAIN) + product(gate_back, gate, PLAIN)

    @pl.when(index == 0)
    def begin():
        shrunk_ref[...] = shrunk
        second_back_ref[...] = second_back

    @pl.when(index > 0)
    def add():
        shrunk_ref[...] += shrunk
        second_back_ref[...] += second_back

    for half in range(2):

        @pl.when(index % 2 == half)
        def send(half=half):
            pair = index // 2

            @pl.when(index >= 2)
            def free():
                for copy in grad_copies(half, pair - 1):
                    copy.wait()

            grads_ref[half, 0] = product(active_back, second, TN).astype(jnp.bfloat16)
            grads_ref[half, 1] = product(gate_back, second, TN).astype(jnp.bfloat16)
            grads_ref[half, 2] = product(hidden, upstream, TN).astype(jnp.bfloat16)
            for copy in grad_copies(half, pair):
                copy.start()

    @pl.when(index == GROUPS - 1)
    def drain():
        for half in range(2):
            for copy in grad_copies(half, 1):
                copy.wait()
        for copy in zero_copies():
            copy.wait()


def feed_forward(second, upstream, pieces):
    count, width = second.shape
    block = (RUNS, 1, UNITS, LANES)
    held = pl.BlockSpec((count, width), lambda i: (0, 0), pipeline_mode=pl.Buffered(1))
    wide = jax.ShapeDtypeStruct((count, width), jnp.float32)
    run = EXPAND_RUN + SHRINK_RUN
    copies = max(
        2 * len(run_segments(half * UNITS, (half + 1) * UNITS, EXPAND_RUN)) for half in range(2)
    ) + len(run_segments(0, UNITS, SHRINK_RUN))
    return pl.pallas_call(
        feed_kernel,
        grid=(GROUPS,),
        in_specs=[
            held,
            held,
            pl.BlockSpec(block, lambda i: (0, i // 2, i % 2, 0)),
            pl.BlockSpec(block, lambda i: (0, i // 2 + 2, i % 2, 0)),
            pl.BlockSpec(block, lambda i: (0, i, 2, 0)),
        ],
        out_specs=[held, held, pl.BlockSpec(memory_space=pl.ANY)],
        out_shape=[wide, wide, jax.ShapeDtypeStruct((RUNS, GROUPS, run, width), jnp.bfloat16)],
        scratch_shapes=[
            pltpu.VMEM((2, 3, UNITS, width), jnp.bfloat16),
            pltpu.VMEM((max(EXPAND_RUN, SHRINK_RUN), width), jnp.bfloat16),
            pltpu.SemaphoreType.DMA((2, copies)),
            pltpu.SemaphoreType.DMA((GROUPS * 8,)),
        ],
        compiler_params=pltpu.CompilerParams(vmem_limit_bytes=VMEM_LIMIT),
        cost_estimate=pl.CostEstimate(
            flops=18 * count * width * FF,
            bytes_accessed=12 * FF * width + 16 * count * width,
            transcendentals=2 * count * FF,
        ),
    )(second, upstream, pieces, pieces, pieces)


def adam_step(rotated, first, second):
    average = BETA_ONE * first + (1.0 - BETA_ONE) * rotated
    variance = BETA_TWO * second + (1.0 - BETA_TWO) * rotated * rotated
    direction = (
        average / (1.0 - BETA_ONE**STEP) / (jnp.sqrt(variance / (1.0 - BETA_TWO**STEP)) + ADAM_EPS)
    )
    return (average, variance, direction)


def body(
    tokens,
    cotangent,
    lengths,
    triple_weight,
    output_weight,
    expand_weight,
    shrink_weight,
    norm_gains,
    side_bases,
    output_right,
    triple_first,
    triple_second,
    output_first,
    output_second,
    expand_first,
    expand_second,
    shrink_first,
    shrink_second,
    gains_first,
    gains_second,
):
    rows_here, local_len, width = tokens.shape
    count = rows_here * local_len
    shards = lax.axis_size("seq")
    groups = lax.axis_size("outer") * lax.axis_size("core")
    phases = HEADS // shards
    piece = width // shards
    fsdp = ("outer", "core")
    everyone = ("seq",) + fsdp
    offset = lax.axis_index("seq") * local_len
    position = offset + jnp.arange(local_len, dtype=jnp.int32)
    cosine, sine = rotary_tables(position)
    every = jnp.arange(shards * local_len, dtype=jnp.int32)
    all_cosine, all_sine = (
        table.reshape(HEAD_DIM // 2, shards, local_len).transpose(1, 0, 2)
        for table in rotary_tables(every)
    )
    valid = (position[None, :] < lengths[:, None]).astype(jnp.float32).reshape(count, 1)
    exchange = functools.partial(lax.all_to_all, axis_name="seq", split_axis=0, concat_axis=0)

    def gathered(shard):
        flat = lax.all_gather(shard, everyone, axis=0, tiled=False)
        return flat.reshape((shards, groups) + shard.shape)

    triple_pieces = gathered(triple_weight.T.astype(jnp.bfloat16))
    output_columns = width // groups
    lanes = min(piece, output_columns)

    def fold(block):
        rows = block.shape[0]
        return block.reshape(rows, -1, lanes).transpose(1, 0, 2).reshape(-1, lanes)

    bases_low = side_bases.astype(jnp.bfloat16)
    right_low = output_right.astype(jnp.bfloat16)
    member = lax.axis_index("outer") * lax.axis_size("core") + lax.axis_index("core")
    base_rows = piece // groups
    flat = tokens.reshape(count, width).astype(jnp.float32)
    first_normed, first_back = jax.vjp(layer_norm, flat, norm_gains[0])
    first_low = first_normed.astype(jnp.bfloat16)
    projected = [
        project_heads(triple_pieces, first_low, cosine, sine, phases, phase)
        for phase in range(phases)
    ]
    triple_rows = [rows for _, rows in projected]
    joints = [exchange(joint) for joint, _ in projected]
    other_shards = jnp.concatenate(
        [
            expand_weight.T.astype(jnp.bfloat16),
            shrink_weight.astype(jnp.bfloat16),
            fold(output_weight.astype(jnp.bfloat16)),
        ],
        axis=0,
    )
    other_shards, joints[0] = lax.optimization_barrier((other_shards, joints[0]))
    other_pieces = gathered(other_shards)
    expand_rows = 2 * FF // groups
    shrink_rows = FF // groups
    output_rows = (
        other_pieces[:, :, expand_rows + shrink_rows :]
        .reshape(shards, groups, output_columns // lanes, phases, HEAD_DIM, lanes)
        .transpose(3, 0, 4, 1, 2, 5)
        .reshape(phases, shards * HEAD_DIM, width)
    )
    canonical = (shards, groups, piece) == (RUNS, GROUPS, LANES)
    if canonical:
        feed_pieces = other_pieces
    else:
        feed_pieces = [
            other_pieces[:, :, start:end]
            .transpose(1, 2, 0, 3)
            .reshape(GROUPS, -1, RUNS, LANES)
            .transpose(2, 0, 1, 3)
            for start, end in ((0, expand_rows), (expand_rows, expand_rows + shrink_rows))
        ]
        feed_pieces = jnp.concatenate(feed_pieces, axis=2)
    chosen = jnp.stack([bases_low[0], bases_low[2], bases_low[3]])
    chosen = lax.dynamic_slice_in_dim(chosen, member * base_rows, base_rows, 1)
    bases_full = gathered(chosen).transpose(2, 0, 1, 3, 4).reshape(3, width, width)

    swap = functools.partial(lax.ppermute, axis_name="core", perm=[(0, 1), (1, 0)])
    both_lengths = jnp.concatenate([lengths, swap(lengths)])
    others = [swap(joint) for joint in joints]
    forwards = [attend_forward(both_lengths, *pair) for pair in zip(joints, others)]
    attends = [
        exchange(
            jnp.stack([outcome[0], swap(outcome[1])], axis=1).reshape(shards, HEAD_DIM, count)
        )
        for outcome, _ in forwards
    ]
    attends = [attend.reshape(shards * HEAD_DIM, count) for attend in attends]
    expand_height = -(-expand_rows // (16 * shards)) * 16
    shrink_height = -(-shrink_rows // (16 * shards)) * 16

    def to_rows(block):
        block = exchange(block)
        return block.transpose(1, 0, 2).reshape(block.shape[1], -1)

    def to_pieces(rows):
        return exchange(rows.reshape(rows.shape[0], shards, -1).transpose(1, 0, 2))

    def padded(block, height):
        block = jnp.pad(block, ((0, height * shards - block.shape[0]), (0, 0)))
        return block.reshape(shards, height, piece)

    def by_phase(block):
        return (
            block.reshape(-1, phases, HEAD_DIM, piece)
            .transpose(1, 0, 2, 3)
            .reshape(phases, shards, -1, piece)
        )

    def from_phases(blocks):
        block = jnp.stack(blocks).astype(jnp.float32).reshape(phases, -1, HEAD_DIM, piece)
        return block.transpose(1, 0, 2, 3).reshape(-1, piece)

    moments = []
    for expand, shrink, triple in (
        (expand_first, shrink_first, triple_first),
        (expand_second, shrink_second, triple_second),
    ):
        moments += [padded(expand.T, expand_height), padded(shrink, shrink_height)]
        moments += list(by_phase(triple.T))
    moments, _ = lax.optimization_barrier((moments, attends[0]))
    heights = [moment.shape[1] for moment in moments]
    moments = to_rows(jnp.concatenate(moments, axis=1))
    edges = [sum(heights[:index]) for index in range(len(heights) + 1)]
    moments = [moments[start:end] for start, end in zip(edges, edges[1:])]
    moments = list(zip(moments[: phases + 2], moments[phases + 2 :]))

    branch = sum(outer_sum(attends[phase], output_rows[phase]) for phase in range(phases))
    middle = flat + branch
    second_normed, second_back = jax.vjp(layer_norm, middle, norm_gains[1])
    second_low = second_normed.astype(jnp.bfloat16)
    upstream = cotangent.reshape(count, width).astype(jnp.float32) * valid
    upstream_low = upstream.astype(jnp.bfloat16)
    shrunk, second_change, parts = feed_forward(second_low, upstream_low, feed_pieces)
    mixed = ((middle + shrunk) * valid).astype(jnp.bfloat16).reshape(tokens.shape)
    second_input, second_gain = second_back(second_change)
    middle_back = upstream + second_input
    branch_low = middle_back.astype(jnp.bfloat16)
    moments, branch_low = lax.optimization_barrier((moments, branch_low))
    attend_backs = [
        exchange(
            back_product(output_rows[phase], branch_low)
            .astype(jnp.bfloat16)
            .reshape(shards, HEAD_DIM, count)
        )
        for phase in range(phases)
    ]

    def cut(product, height):
        block = product.reshape(groups, -1, width)
        block = jnp.pad(block, ((0, 0), (0, height * shards - block.shape[1]), (0, 0)))
        return block.reshape(groups, shards, height, width)

    if not canonical:
        parts = parts.transpose(1, 0, 2, 3)
        parts = [
            cut(block.reshape(GROUPS, -1, width)[:, : size // GROUPS], height)
            for block, size, height in (
                (parts[:, :, :EXPAND_RUN], 2 * FF, expand_height),
                (parts[:, :, EXPAND_RUN:], FF, shrink_height),
            )
        ]
        parts = jnp.concatenate(parts, axis=2).transpose(1, 0, 2, 3)
    parts = parts.reshape(shards * groups, -1, width)
    owned = lax.psum_scatter(parts, everyone, scatter_dimension=0, tiled=False)
    feed_height = expand_height + shrink_height

    def shared_sum(blocks):
        core = lax.axis_index("core")
        mine = lax.dynamic_index_in_dim(blocks, core, 1, keepdims=False)
        other = lax.dynamic_index_in_dim(blocks, 1 - core, 1, keepdims=False)
        both = (mine.astype(jnp.float32) + swap(other).astype(jnp.float32)).astype(jnp.bfloat16)
        both = both.swapaxes(0, 1).reshape((-1,) + both.shape[2:])
        terms = lax.all_to_all(both, ("seq", "outer"), 0, 0)
        return jnp.sum(terms.astype(jnp.float32), axis=0).astype(jnp.bfloat16)

    outer = lax.axis_size("outer")
    output_part = jnp.stack(
        [
            jnp.dot(attend, branch_low, preferred_element_type=jnp.float32)
            .astype(jnp.bfloat16)
            .reshape(shards, HEAD_DIM, width)
            for attend in attends
        ],
        axis=1,
    )
    output_low = shared_sum(
        output_part.reshape(shards, piece, outer, -1, output_columns).transpose(2, 3, 0, 1, 4)
    )

    def soap_rows(rows, base, moment):
        rotated = plain_product(rows, base)
        direction = adam_step(rotated, *moment)[2]
        step = back_product(direction.astype(jnp.bfloat16), base)
        return rotated.astype(jnp.bfloat16), step.astype(jnp.bfloat16)

    expand_turns, expand_steps = soap_rows(owned[:expand_height], bases_full[1], moments[0])
    shrink_turns, shrink_steps = soap_rows(
        owned[expand_height:feed_height], bases_full[2], moments[1]
    )
    settled = to_pieces(
        jnp.concatenate(
            [owned[:feed_height], expand_turns, shrink_turns, expand_steps, shrink_steps]
        )
    )

    output_left = exchange(
        outer_sum(bases_low[1], output_low).astype(jnp.bfloat16).reshape(shards, piece, -1)
    )
    output_left = jnp.sum(output_left.astype(jnp.float32), axis=0).astype(jnp.bfloat16)
    output_turned = plain_product(output_left, right_low).astype(jnp.bfloat16)
    output_turned = lax.all_to_all(
        output_turned.reshape(piece, groups, output_columns).transpose(1, 0, 2), fsdp, 0, 0
    )
    output_turned = jnp.sum(output_turned.astype(jnp.float32), axis=0)
    other_backs = [swap(attend_back) for attend_back in attend_backs]
    grads = []
    for phase in range(phases):
        own_grad, other_grad = attend_backward(
            both_lengths,
            joints[phase],
            others[phase],
            attend_backs[phase],
            other_backs[phase],
            *forwards[phase],
            all_cosine,
            all_sine,
        )
        grad = own_grad.astype(jnp.float32) + swap(other_grad).astype(jnp.float32)
        grads.append(exchange(grad.astype(jnp.bfloat16)))
    joint_backs = []
    triple_lows, triple_turns, triple_steps = [], [], []
    for phase in range(phases):
        if phase == phases - 1:
            earlier = (triple_lows, triple_turns, triple_steps, settled, output_turned)
            earlier, grads[phase] = lax.optimization_barrier((earlier, grads[phase]))
            triple_lows, triple_turns, triple_steps, settled, output_turned = earlier
        joint_backs.append(grads[phase].reshape(shards * 3 * HEAD_DIM, count))
        part = jnp.dot(joint_backs[phase], first_low, preferred_element_type=jnp.float32)
        part = part.astype(jnp.bfloat16).reshape(shards, 3, HEAD_DIM, width).transpose(1, 0, 2, 3)
        rows = shared_sum(part.reshape(outer, -1, shards, part.size // (width * shards * groups), width))
        turns, steps = soap_rows(rows, bases_full[0], moments[2 + phase])
        low, turned, step = jnp.split(to_pieces(jnp.concatenate([rows, turns, steps])), 3, axis=1)
        triple_lows.append(low)
        triple_turns.append(turned)
        triple_steps.append(step)

    def settled_piece(start, height, size):
        return settled[:, start : start + height].reshape(-1, piece)[:size].astype(jnp.float32)

    expand_gradient, expand_turned_grad, expand_back = (
        settled_piece(index * feed_height, expand_height, expand_rows).T for index in range(3)
    )
    shrink_gradient, shrink_turned_grad, shrink_back = (
        settled_piece(index * feed_height + expand_height, shrink_height, shrink_rows)
        for index in range(3)
    )
    expand_average, expand_variance, _ = adam_step(expand_turned_grad, expand_first, expand_second)
    shrink_average, shrink_variance, _ = adam_step(shrink_turned_grad, shrink_first, shrink_second)
    output_average, output_variance, output_direction = adam_step(
        output_turned, output_first, output_second
    )
    output_wide = lax.all_gather(output_direction.astype(jnp.bfloat16), fsdp, axis=1, tiled=True)
    output_middle = back_product(output_wide, right_low).astype(jnp.bfloat16)
    output_back = plain_product(
        bases_low[1], lax.all_gather(output_middle, "seq", axis=0, tiled=True)
    )
    triple_turned = from_phases(triple_turns).T
    triple_back = from_phases(triple_steps).T
    triple_gradient = from_phases(triple_lows).T
    triple_average, triple_variance, _ = adam_step(triple_turned, triple_first, triple_second)
    first_input, first_gain = first_back(
        sum(
            outer_sum(joint_backs[phase], triple_rows[phase].reshape(-1, width))
            for phase in range(phases)
        )
    )
    token_gradient = (middle_back + first_input).astype(jnp.bfloat16).reshape(tokens.shape)
    gains_gradient = jnp.stack([first_gain, second_gain])
    for axis in ("core", "outer", "seq"):
        members = range(lax.axis_size(axis))
        for step in range(len(members).bit_length() - 1):
            pairs = [(member, member ^ (1 << step)) for member in members]
            gains_gradient = gains_gradient + lax.ppermute(gains_gradient, axis, pairs)
    gains_average, gains_variance, gains_direction = adam_step(
        gains_gradient, gains_first, gains_second
    )
    output_gradient = output_low.astype(jnp.float32)
    triple_updated = (triple_weight - WEIGHT_RATES[0] * triple_back) * (
        1.0 - WEIGHT_RATES[0] * DECAY_RATE
    )
    output_updated = (output_weight - WEIGHT_RATES[1] * output_back) * (
        1.0 - WEIGHT_RATES[1] * DECAY_RATE
    )
    expand_updated = (expand_weight - WEIGHT_RATES[2] * expand_back) * (
        1.0 - WEIGHT_RATES[2] * DECAY_RATE
    )
    shrink_updated = (shrink_weight - WEIGHT_RATES[3] * shrink_back) * (
        1.0 - WEIGHT_RATES[3] * DECAY_RATE
    )
    gains_updated = norm_gains - GAINS_RATE * gains_direction
    return (
        mixed,
        token_gradient,
        triple_gradient,
        output_gradient,
        expand_gradient,
        shrink_gradient,
        gains_gradient,
        triple_average,
        triple_variance,
        triple_updated,
        triple_updated.astype(jnp.bfloat16),
        output_average,
        output_variance,
        output_updated,
        output_updated.astype(jnp.bfloat16),
        expand_average,
        expand_variance,
        expand_updated,
        expand_updated.astype(jnp.bfloat16),
        shrink_average,
        shrink_variance,
        shrink_updated,
        shrink_updated.astype(jnp.bfloat16),
        gains_average,
        gains_variance,
        gains_updated,
    )


def solution(mesh):
    in_specs = (
        P(("outer", "core"), "seq", None),
        P(("outer", "core"), "seq", None),
        P(("outer", "core")),
        P("seq", ("outer", "core")),
        P("seq", ("outer", "core")),
        P("seq", ("outer", "core")),
        P(("outer", "core"), "seq"),
        P(),
        P(None, "seq", None),
        P(("outer", "core"), None),
        P("seq", ("outer", "core")),
        P("seq", ("outer", "core")),
        P("seq", ("outer", "core")),
        P("seq", ("outer", "core")),
        P("seq", ("outer", "core")),
        P("seq", ("outer", "core")),
        P(("outer", "core"), "seq"),
        P(("outer", "core"), "seq"),
        P(),
        P(),
    )
    out_specs = (
        P(("outer", "core"), "seq", None),
        P(("outer", "core"), "seq", None),
        P("seq", ("outer", "core")),
        P("seq", ("outer", "core")),
        P("seq", ("outer", "core")),
        P(("outer", "core"), "seq"),
        P(),
        P("seq", ("outer", "core")),
        P("seq", ("outer", "core")),
        P("seq", ("outer", "core")),
        P("seq", ("outer", "core")),
        P("seq", ("outer", "core")),
        P("seq", ("outer", "core")),
        P("seq", ("outer", "core")),
        P("seq", ("outer", "core")),
        P("seq", ("outer", "core")),
        P("seq", ("outer", "core")),
        P("seq", ("outer", "core")),
        P("seq", ("outer", "core")),
        P(("outer", "core"), "seq"),
        P(("outer", "core"), "seq"),
        P(("outer", "core"), "seq"),
        P(("outer", "core"), "seq"),
        P(),
        P(),
        P(),
    )
    groups = mesh.shape["fsdp"]
    devices = mesh.devices.reshape(mesh.shape["seq"], groups // 2, 2)
    split = Mesh(devices, ("seq", "outer", "core"))
    return jax.shard_map(body, mesh=split, in_specs=in_specs, out_specs=out_specs, check_vma=False)
```

time: 3950 us -> 1360 us (0.34)
  matrix products: 1620 us -> 60.4 us
  waiting for transfers between devices: 1650 us -> 497 us
  Pallas kernels: 0 us -> 408 us
  other arithmetic: 277 us -> 88.1 us
  local copies, waits for them, and re-layouts: 258 us -> 103 us
  starting transfers between devices: 1.41 us -> 125 us
  blocking collectives: 106 us -> 53.8 us
    dot_general x60 -> x4, matrix products: 1470 us -> 16.1 us  [the longest x2 11.5 us: body(): jnp.dot(joint_backs[phase], first_low, preferred_element_type=jnp.float32)]
    reduce_scatter x9 -> x1, waiting for transfers between devices: 872 us -> 0.01 us  [body(): owned = lax.psum_scatter(parts, everyone, scatter_dimension=0, tiled=False)]
    all_gather x10 -> x3, waiting for transfers between devices: 493 us -> 69.2 us  [gathered(): flat = lax.all_gather(shard, everyone, axis=0, tiled=False)]
    all_to_all x0 -> x17, waiting for transfers between devices: none -> 423 us  [the longest x2 124 us: body(): joints = [exchange(joint) for joint, _ in projected]]
    pallas_call x0 -> x7, Pallas kernels: none -> 408 us  [the longest x2 232 us: attend_backward(): pl.pallas_call(backward_kernel, grid=(2, shards), in_specs=[pl.BlockSpec(...]
    unnamed x31 -> x4, waiting for transfers between devices: 284 us -> 0.07 us
    reduce_sum x9 -> x5, other arithmetic: 175 us -> 5.71 us  [the longest x3 3.6 us: shared_sum(): return jnp.sum(terms.astype(jnp.float32), axis=0).astype(jnp.bfloat16)]
    all_to_all x0 -> x17, starting transfers between devices: none -> 118 us  [the longest x3 33.7 us: shared_sum(): terms = lax.all_to_all(both, ('seq', 'outer'), 0, 0)]
  transfers between devices with their start and end apart: 25 -> 38, of which waited for: 16 -> 17; matrix products, arithmetic and copies ran while one was open for 52% -> 16% of each run, Pallas kernels for 0% -> 30%
where the time goes in v1:
time: 1360 us; the launch traced here: 1350 us
  waiting for transfers between devices  497 us (37%)
  Pallas kernels  408 us (30%)
  starting transfers between devices  125 us (9%)
  local copies, waits for them, and re-layouts  103 us (8%)
  other arithmetic  88.1 us (6%)
  matrix products  60.4 us (4%)
  blocking collectives  53.8 us (4%)
  between operations  16 us (1%)
    pallas_call x2, Pallas kernels, attend_backward(): pl.pallas_call(backward_kernel, grid=(2, shards), in_specs=[pl.BlockSpec(...  232 us
    all_to_all x2, waiting for transfers between devices, body(): joints = [exchange(joint) for joint, _ in projected]  124 us
    all_to_all x2, waiting for transfers between devices, body(): grads.append(exchange(grad.astype(jnp.bfloat16)))  120 us
    pallas_call x2, Pallas kernels, attend_forward(): pl.pallas_call(forward_kernel, grid=(2, half), in_specs=[pl.BlockSpec(mem...  91.3 us
    pallas_call x1, Pallas kernels, feed_forward(): pl.pallas_call(feed_kernel, grid=(GROUPS,), in_specs=[held, held, pl.Bloc...  70.9 us
    all_gather x3, waiting for transfers between devices, gathered(): flat = lax.all_gather(shard, everyone, axis=0, tiled=False)  69.2 us
    all_to_all x2, waiting for transfers between devices, body(): exchange(jnp.stack([outcome[0], swap(outcome[1])], axis=1).reshape(shards...  55.3 us
    all_to_all x3, waiting for transfers between devices, shared_sum(): terms = lax.all_to_all(both, ('seq', 'outer'), 0, 0)  53.1 us
  transfers between devices with their start and end apart: 38, of which 17 were waited for; matrix products, arithmetic and copies ran while one was open for 16% of the time, Pallas kernels for 30%

profile of v1, /device:TPU:0, one launch (start us, length us, event | category | flops | bytes accessed | tf_op | source)
XLA Modules:
  0.0 1351.5 jit_solution(1616974249923515720)
XLA Ops:
  15.7 69.2 %all-gather.7.cloned.1.call-done = bf16[24576,128]{0,1:T(8,128)(2,1)} async-done(((bf16[768,128]{0,1:T(8,128)(2,1)}), bf16[24576,128]{0,1:T(8,128)(2,1)}) %all-gather.7.cloned.1.call-update) | async-done | bytes 6291472 | tf_op jit(solution)/shard_map/all_gather | solution.py:635
  84.9 8.6 copy.115
  93.5 7.1 shard_map.395
  100.7 4.6 all-to-all-start
  106.3 70.4 %all-to-all-done.own_ref = bf16[8,192,1024]{2,1,0:T(8,128)(2,1)} async-done(((bf16[8,192,1024]{2,1,0:T(8,128)(2,1)}), bf16[8,192,1024]{2,1,0:T(8,128)(2,1)}, u32[]{:S(2)}, u32[]{:S(2)}) %all-to-all-start) | async-done | bytes 3145760 | tf_op jit(solution)/shard_map/all_to_all | solution.py:658
  176.7 7.2 shard_map.397
  183.9 4.4 all-to-all-start.2
  191.1 45.6 %shard_map.396 = (bf16[2,4,64,1024]{3,2,1,0:T(8,128)(2,1)}, f32[2,4,1,1024]{3,2,1,0:T(1,128)}) custom-call(s32[2]{0:T(128)} %pad_add_fusion.length_ref, bf16[8,192,1024]{2,1,0:T(8,128)(2,1)} %all-to-all-done.own_ref, bf16[8,192,1024]{2,1,0:T(8,128)(2,1)} %collective-permute-done.1.other_ref), custom_call_target="tpu_custom_call" | custom-call | flops 42949672960 | bytes 8388608 | tf_op jit(solution)/shard_map/pallas_call | solution.py:243
  239.1 53.6 %all-to-all-done.2.own_ref = bf16[8,192,1024]{2,1,0:T(8,128)(2,1)} async-done(((bf16[8,192,1024]{2,1,0:T(8,128)(2,1)}), bf16[8,192,1024]{2,1,0:T(8,128)(2,1)}, u32[]{:S(2)}, u32[]{:S(2)}) %all-to-all-start.2) | async-done | bytes 3145760 | tf_op jit(solution)/shard_map/all_to_all | solution.py:658
  293.9 4.0 all-to-all-start.1
  309.4 43.3 %all-to-all-done.1 = bf16[8,64,1024]{2,1,0:T(8,128)(2,1)S(1)} async-done(((bf16[8,64,1024]{2,1,0:T(8,128)(2,1)}), bf16[8,64,1024]{2,1,0:T(8,128)(2,1)S(1)}, u32[]{:S(2)}, u32[]{:S(2)}) %all-to-all-start.1) | async-done | bytes 1048608 | tf_op jit(solution)/shard_map/all_to_all | solution.py:698
  363.1 4.4 all-to-all-start.4
  370.6 45.6 %shard_map.398 = (bf16[2,4,64,1024]{3,2,1,0:T(8,128)(2,1)}, f32[2,4,1,1024]{3,2,1,0:T(1,128)}) custom-call(s32[2]{0:T(128)} %pad_add_fusion.length_ref, bf16[8,192,1024]{2,1,0:T(8,128)(2,1)} %all-to-all-done.2.own_ref, bf16[8,192,1024]{2,1,0:T(8,128)(2,1)} %collective-permute-done.3.other_ref), custom_call_target="tpu_custom_call" | custom-call | flops 42949672960 | bytes 8388608 | tf_op jit(solution)/shard_map/pallas_call | solution.py:243
  419.2 3.4 fusion.16.upstream_ref
  424.9 11.1 all-to-all-done.4
  435.9 4.2 all-to-all-start.3
  454.2 2.6 squeeze.43
  456.8 2.7 squeeze.45
  459.5 4.5 fusion.138
  464.0 12.1 all-to-all-done.3
  476.1 4.4 fusion.134
  484.3 70.9 %shard_map.399 = (f32[1024,1024]{1,0:T(8,128)}, f32[1024,1024]{1,0:T(8,128)}, bf16[8,4,272,1024]{3,2,1,0:T(8,128)(2,1)}) custom-call(bf16[1024,1024]{1,0:T(8,128)(2,1)} %multiply_convert_fusion.1.second_ref, bf16[1024,1024]{1,0:T(8,128)(2,1)} %fusion.16.upstream_ref, bf16[8,4,2224,128]{3,2,1,0:T(8,128)(2,1)} %bitcast.400, ...), custom_call_target="tpu_custom_call" | custom-call | flops 49526341632 | bytes 49020928 | tf_op jit(solution)/shard_map/pallas_call | solution.py:557
  555.2 5.2 multiply_reduce_fusion
  561.1 4.9 fusion.124
  570.4 4.4 all-to-all-start.5
  574.8 4.9 multiply_sine_fusion
  579.6 20.7 %all-to-all-done.5.own_back_ref = bf16[8,64,1024]{2,1,0:T(8,128)(2,1)} async-done(((bf16[8,64,1024]{2,1,0:T(8,128)(2,1)}), bf16[8,64,1024]{2,1,0:T(8,128)(2,1)}, u32[]{:S(2)}, u32[]{:S(2)}) %all-to-all-start.5) | async-done | bytes 1048608 | tf_op jit(solution)/shard_map/all_to_all | solution.py:756
  600.3 3.9 convolution_convert_fusion.2
  604.2 4.2 all-to-all-start.13
  608.5 3.3 convolution_convert_fusion.3
  614.6 3.3 reshape.428
  617.9 115.9 %shard_map.400 = (bf16[8,192,1024]{2,1,0:T(8,128)(2,1)}, bf16[8,192,1024]{2,1,0:T(8,128)(2,1)}) custom-call(s32[2]{0:T(128)} %pad_add_fusion.length_ref, bf16[8,192,1024]{2,1,0:T(8,128)(2,1)} %all-to-all-done.own_ref, bf16[8,192,1024]{2,1,0:T(8,128)(2,1)} %collective-permute-done.1.other_ref, bf16[8,64,1024]{2,1,0:T(8,128)(2,1)} %all-to-all-done.5.own_back_ref, ...), custom_call_target="tpu_custom_call" | custom-call | flops 111669149696 | bytes 20971520 | tf_op jit(solution)/shard_map/pallas_call | solution.py:391
  734.4 4.3 convert_bitcast_fusion.1
  740.1 2.6 collective-permute-done.8
  745.4 23.0 %all-to-all-start.10 = ((bf16[16,128,256]{2,1,0:T(8,128)(2,1)}), bf16[16,128,256]{2,1,0:T(8,128)(2,1)S(1)}, u32[]{:S(2)}, u32[]{:S(2)}) async-start(bf16[16,128,256]{2,1,0:T(8,128)(2,1)} %bitcast.76), calls=%async_computation.11 | async-start | bytes 2097152 | tf_op jit(solution)/shard_map/all_to_all | solution.py:789
  768.4 6.2 add_convert_fusion.1
  774.6 25.8 %all-to-all-done.10 = bf16[16,128,256]{2,1,0:T(8,128)(2,1)S(1)} async-done(((bf16[16,128,256]{2,1,0:T(8,128)(2,1)}), bf16[16,128,256]{2,1,0:T(8,128)(2,1)S(1)}, u32[]{:S(2)}, u32[]{:S(2)}) %all-to-all-start.10) | async-done | bytes 1048608 | tf_op jit(solution)/shard_map/all_to_all | solution.py:789
  800.4 9.8 all-to-all-start.6
  812.9 73.7 %all-to-all-done.6 = bf16[8,192,1024]{2,1,0:T(8,128)(2,1)} async-done(((bf16[8,192,1024]{2,1,0:T(8,128)(2,1)}), bf16[8,192,1024]{2,1,0:T(8,128)(2,1)}, u32[]{:S(2)}, u32[]{:S(2)}) %all-to-all-start.6) | async-done | bytes 3145760 | tf_op jit(solution)/shard_map/all_to_all | solution.py:845
  886.5 4.2 all-to-all-start.11
  890.7 5.8 convolution_convert_fusion.1
  900.0 115.7 %shard_map.401 = (bf16[8,192,1024]{2,1,0:T(8,128)(2,1)}, bf16[8,192,1024]{2,1,0:T(8,128)(2,1)}) custom-call(s32[2]{0:T(128)} %pad_add_fusion.length_ref, bf16[8,192,1024]{2,1,0:T(8,128)(2,1)} %all-to-all-done.2.own_ref, bf16[8,192,1024]{2,1,0:T(8,128)(2,1)} %collective-permute-done.3.other_ref, bf16[8,64,1024]{2,1,0:T(8,128)(2,1)} %all-to-all-done.13.own_back_ref, ...), custom_call_target="tpu_custom_call" | custom-call | flops 111669149696 | bytes 20971520 | tf_op jit(solution)/shard_map/pallas_call | solution.py:391
  1018.3 19.4 %all-to-all-start.12 = ((bf16[4,128,256]{2,1,0:T(8,128)(2,1)}), bf16[4,128,256]{2,1,0:T(8,128)(2,1)S(1)}, u32[]{:S(2)}, u32[]{:S(2)}) async-start(bf16[4,128,256]{2,1,0:T(8,128)(2,1)} %bitcast.380), calls=%async_computation.13 | async-start | bytes 524288 | tf_op jit(solution)/shard_map/all_to_all | solution.py:827
  1037.7 2.6 fusion.24
  1043.7 6.1 all-to-all-start.7
  1049.9 6.1 add_convert_fusion
  1056.0 27.3 %all-to-all-done.7 = bf16[16,48,1024]{2,1,0:T(8,128)(2,1)} async-done(((bf16[16,48,1024]{2,1,0:T(8,128)(2,1)}), bf16[16,48,1024]{2,1,0:T(8,128)(2,1)}, u32[]{:S(2)}, u32[]{:S(2)}) %all-to-all-start.7) | async-done | bytes 1572896 | tf_op jit(solution)/shard_map/all_to_all | solution.py:789
  1083.3 8.1 all-to-all-start.14
  1091.5 5.9 fusion.125
  1114.6 45.9 %all-to-all-done.14 = bf16[8,192,1024]{2,1,0:T(8,128)(2,1)} async-done(((bf16[8,192,1024]{2,1,0:T(8,128)(2,1)}), bf16[8,192,1024]{2,1,0:T(8,128)(2,1)}, u32[]{:S(2)}, u32[]{:S(2)}) %all-to-all-start.14) | async-done | bytes 3145760 | tf_op jit(solution)/shard_map/all_to_all | solution.py:845
  1160.5 4.1 all-to-all-start.8
  1164.6 2.9 fusion.28
  1168.2 5.8 all-to-all-done.8
  1174.0 4.7 all-to-all-start.9
  1185.6 31.4 %all-to-all-done.9 = bf16[8,816,128]{2,1,0:T(8,128)(2,1)} async-done(((bf16[8,816,128]{2,1,0:T(8,128)(2,1)}), bf16[8,816,128]{2,1,0:T(8,128)(2,1)}, u32[]{:S(2)}, u32[]{:S(2)}) %all-to-all-start.9) | async-done | bytes 1671200 | tf_op jit(solution)/shard_map/all_to_all | solution.py:712
  1217.0 5.8 convolution_convert_fusion
  1225.0 5.7 fusion.139
  1230.7 6.3 fusion.11
  1240.9 6.7 all_gather.30
  1255.5 4.5 all-to-all-start.15
  1264.6 5.6 fusion.21
  1272.4 47.1 %all_gather.31 = bf16[1024,256]{1,0:T(8,128)(2,1)S(1)} all-gather(bf16[128,256]{1,0:T(8,128)(2,1)S(1)} %convolution_convert_fusion.12), channel_id=1, replica_groups=mesh['seq'=8,'outer'=2,'core'=2] {'seq'}, dimensions={0}, use_global_device_ids=true | all-gather | bytes 589824 | tf_op jit(solution)/shard_map/all_gather | solution.py:881
  1327.1 3.8 all-to-all-start.16
  1332.5 2.9 collective-permute-start.16
  (334 shorter events, 151.4 us)
Async XLA Ops:
  7.2 77.6 %all-gather.7.cloned.1.call-start = ((), (), s32[]{:S(2)}) async-start(), calls=%async_computation.19 | async-start | bytes 6488064 | tf_op jit(solution)/shard_map/all_gather | solution.py:635
  100.7 76.0 %all-to-all-start = ((bf16[8,192,1024]{2,1,0:T(8,128)(2,1)}), bf16[8,192,1024]{2,1,0:T(8,128)(2,1)}, u32[]{:S(2)}, u32[]{:S(2)}) async-start(bf16[8,192,1024]{2,1,0:T(8,128)(2,1)} %get-tuple-element.66), calls=%async_computation | async-start | bytes 6291456 | tf_op jit(solution)/shard_map/all_to_all | solution.py:658
  105.2 342.6 %all-gather.9.cloned.1.call-start = ((), (), s32[]{:S(2)}) async-start(), calls=%async_computation.20 | async-start | bytes 18788352 | tf_op jit(solution)/shard_map/all_gather | solution.py:635
  176.7 14.5 %collective-permute-start.1 = (bf16[8,192,1024]{2,1,0:T(8,128)(2,1)}, bf16[8,192,1024]{2,1,0:T(8,128)(2,1)}, u32[]{:S(2)}, u32[]{:S(2)}) collective-permute-start(bf16[8,192,1024]{2,1,0:T(8,128)(2,1)} %all-to-all-done.own_ref), channel_id=1, source_target_pairs={{0,1},{1,0},{2,3},{3,2},{4,5},{5,4},{6,7},{7,6},{8,9},{9,8},{10,11... | collective-permute-start | bytes 9437192 | tf_op jit(solution)/shard_map/ppermute | solution.py:695
  183.9 108.8 %all-to-all-start.2 = ((bf16[8,192,1024]{2,1,0:T(8,128)(2,1)}), bf16[8,192,1024]{2,1,0:T(8,128)(2,1)}, u32[]{:S(2)}, u32[]{:S(2)}) async-start(bf16[8,192,1024]{2,1,0:T(8,128)(2,1)} %get-tuple-element.70), calls=%async_computation.2 | async-start | bytes 6291456 | tf_op jit(solution)/shard_map/all_to_all | solution.py:658
  188.4 1.5 collective-permute-start
  238.9 53.9 %collective-permute-start.2 = (bf16[4,64,1024]{2,1,0:T(8,128)(2,1)}, bf16[4,64,1024]{2,1,0:T(8,128)(2,1)S(1)}, u32[]{:S(2)}, u32[]{:S(2)}) collective-permute-start(bf16[4,64,1024]{2,1,0:T(8,128)(2,1)} %get-tuple-element.228), channel_id=1, source_target_pairs={{0,1},{1,0},{2,3},{3,2},{4,5},{5,4},{6,7},{7,6},{8,9},{9,8},{10,11... | collective-permute-start | bytes 1572872 | tf_op jit(solution)/shard_map/ppermute | solution.py:699
  292.7 77.8 %collective-permute-start.3 = (bf16[8,192,1024]{2,1,0:T(8,128)(2,1)}, bf16[8,192,1024]{2,1,0:T(8,128)(2,1)}, u32[]{:S(2)}, u32[]{:S(2)}) collective-permute-start(bf16[8,192,1024]{2,1,0:T(8,128)(2,1)} %all-to-all-done.2.own_ref), channel_id=1, source_target_pairs={{0,1},{1,0},{2,3},{3,2},{4,5},{5,4},{6,7},{7,6},{8,9},{9,8},{10,11... | collective-permute-start | bytes 9437192 | tf_op jit(solution)/shard_map/ppermute | solution.py:695
  293.9 58.8 %all-to-all-start.1 = ((bf16[8,64,1024]{2,1,0:T(8,128)(2,1)}), bf16[8,64,1024]{2,1,0:T(8,128)(2,1)S(1)}, u32[]{:S(2)}, u32[]{:S(2)}) async-start(bf16[8,64,1024]{2,1,0:T(8,128)(2,1)} %bitcast.363), calls=%async_computation.1 | async-start | bytes 2097152 | tf_op jit(solution)/shard_map/all_to_all | solution.py:698
  299.2 10.3 copy-start.17
  352.7 9.7 copy-start.39
  363.1 72.8 %all-to-all-start.4 = ((f32[8,736,128]{2,1,0:T(8,128)}), f32[8,736,128]{2,1,0:T(8,128)}, u32[]{:S(2)}, u32[]{:S(2)}) async-start(f32[8,736,128]{2,1,0:T(8,128)} %constant_dynamic-update-slice_fusion), calls=%async_computation.4 | async-start | bytes 6029312 | tf_op jit(solution)/shard_map/all_to_all | solution.py:708
  367.6 723.9 %all-gather.11.cloned.1.call-start = ((), (), s32[]{:S(2)}) async-start(), calls=%async_computation.21 | async-start | bytes 6488064 | tf_op jit(solution)/shard_map/all_gather | solution.py:635
  370.5 47.9 %copy-start.26 = (bf16[2,128,1024]{2,1,0:T(8,128)(2,1)S(1)}, bf16[2,128,1024]{2,1,0:T(8,128)(2,1)}, u32[]{:S(2)}) copy-start(bf16[2,128,1024]{2,1,0:T(8,128)(2,1)} %slice.215) | copy-start | bytes 1572868
  418.4 4.2 collective-permute-start.4
  419.2 146.8 %copy-start.56 = (f32[1024]{0:T(1024)}, f32[1024]{0:T(1024)S(1)}, u32[]{:S(2)}) copy-start(f32[1024]{0:T(1024)S(1)} %fusion.94) | copy-start | bytes 12292
  435.9 40.1 %all-to-all-start.3 = ((bf16[8,64,1024]{2,1,0:T(8,128)(2,1)}), bf16[8,64,1024]{2,1,0:T(8,128)(2,1)}, u32[]{:S(2)}, u32[]{:S(2)}) async-start(bf16[8,64,1024]{2,1,0:T(8,128)(2,1)} %bitcast.362), calls=%async_computation.3 | async-start | bytes 2097152 | tf_op jit(solution)/shard_map/all_to_all | solution.py:698
  570.4 30.0 %copy-start.14 = (bf16[512,1024]{1,0:T(8,128)(2,1)S(1)}, bf16[512,1024]{1,0:T(8,128)(2,1)}, u32[]{:S(2)}) copy-start(bf16[512,1024]{1,0:T(8,128)(2,1)} %squeeze.45) | copy-start | bytes 3145732
  570.4 30.0 %all-to-all-start.5 = ((bf16[8,64,1024]{2,1,0:T(8,128)(2,1)}), bf16[8,64,1024]{2,1,0:T(8,128)(2,1)}, u32[]{:S(2)}, u32[]{:S(2)}) async-start(bf16[8,64,1024]{2,1,0:T(8,128)(2,1)} %bitcast.45), calls=%async_computation.5 | async-start | bytes 2097152 | tf_op jit(solution)/shard_map/all_to_all | solution.py:756
  600.3 17.6 %collective-permute-start.5 = (bf16[8,64,1024]{2,1,0:T(8,128)(2,1)}, bf16[8,64,1024]{2,1,0:T(8,128)(2,1)}, u32[]{:S(2)}, u32[]{:S(2)}) collective-permute-start(bf16[8,64,1024]{2,1,0:T(8,128)(2,1)} %all-to-all-done.5.own_back_ref), channel_id=1, source_target_pairs={{0,1},{1,0},{2,3},{3,2},{4,5},{5,4},{6,7},{7,6},{8,9},{9,8},{10,11... | collective-permute-start | bytes 3145736 | tf_op jit(solution)/shard_map/ppermute | solution.py:831
  604.2 141.2 %all-to-all-start.13 = ((bf16[8,64,1024]{2,1,0:T(8,128)(2,1)}), bf16[8,64,1024]{2,1,0:T(8,128)(2,1)}, u32[]{:S(2)}, u32[]{:S(2)}) async-start(bf16[8,64,1024]{2,1,0:T(8,128)(2,1)} %bitcast.80), calls=%async_computation.14 | async-start | bytes 2097152 | tf_op jit(solution)/shard_map/all_to_all | solution.py:756
  608.5 496.0 %reduce-scatter.2.cloned.1.call-start = ((), (), s32[]{:S(2)}) async-start(), calls=%async_computation.18 | async-start | bytes 18382848 | tf_op jit(solution)/shard_map/reduce_scatter | solution.py:780
  733.8 34.6 %collective-permute-start.6 = (bf16[8,192,1024]{2,1,0:T(8,128)(2,1)}, bf16[8,192,1024]{2,1,0:T(8,128)(2,1)}, u32[]{:S(2)}, u32[]{:S(2)}) collective-permute-start(bf16[8,192,1024]{2,1,0:T(8,128)(2,1)} %get-tuple-element.85), channel_id=1, source_target_pairs={{0,1},{1,0},{2,3},{3,2},{4,5},{5,4},{6,7},{7,6},{8,9},{9,8},{10,11... | collective-permute-start | bytes 9437192 | tf_op jit(solution)/shard_map/ppermute | solution.py:844
  740.0 2.7 collective-permute-start.8
  745.4 55.0 %all-to-all-start.10 = ((bf16[16,128,256]{2,1,0:T(8,128)(2,1)}), bf16[16,128,256]{2,1,0:T(8,128)(2,1)S(1)}, u32[]{:S(2)}, u32[]{:S(2)}) async-start(bf16[16,128,256]{2,1,0:T(8,128)(2,1)} %bitcast.76), calls=%async_computation.11 | async-start | bytes 2097152 | tf_op jit(solution)/shard_map/all_to_all | solution.py:789
  800.4 86.1 %all-to-all-start.6 = ((bf16[8,192,1024]{2,1,0:T(8,128)(2,1)}), bf16[8,192,1024]{2,1,0:T(8,128)(2,1)}, u32[]{:S(2)}, u32[]{:S(2)}) async-start(bf16[8,192,1024]{2,1,0:T(8,128)(2,1)} %add_convert_fusion.1), calls=%async_computation.6 | async-start | bytes 6291456 | tf_op jit(solution)/shard_map/all_to_all | solution.py:845
  810.2 80.5 %copy-start.3 = (bf16[1,1024,1024]{2,1,0:T(8,128)(2,1)S(1)}, bf16[1,1024,1024]{2,1,0:T(8,128)(2,1)}, u32[]{:S(2)}) copy-start(bf16[1,1024,1024]{2,1,0:T(8,128)(2,1)} %param.20) | copy-start | bytes 6291460
  810.2 80.5 %copy-start.59 = (f32[1024]{0:T(1024)S(1)}, f32[1024]{0:T(1024)}, u32[]{:S(2)}) copy-start(f32[1024]{0:T(1024)} %copy-done.58) | copy-start | bytes 12292
  810.2 80.5 %copy-start.61 = (f32[1024]{0:T(1024)S(1)}, f32[1024]{0:T(1024)}, u32[]{:S(2)}) copy-start(f32[1024]{0:T(1024)} %copy-done.60) | copy-start | bytes 12292
  810.2 80.5 %copy-start.63 = (f32[1,1024]{1,0:T(1,128)S(1)}, f32[1,1024]{1,0:T(1,128)}, u32[]{:S(2)}) copy-start(f32[1,1024]{1,0:T(1,128)} %copy-done.62) | copy-start | bytes 12292
  810.3 89.7 %collective-permute-start.9 = (bf16[8,64,1024]{2,1,0:T(8,128)(2,1)}, bf16[8,64,1024]{2,1,0:T(8,128)(2,1)}, u32[]{:S(2)}, u32[]{:S(2)}) collective-permute-start(bf16[8,64,1024]{2,1,0:T(8,128)(2,1)} %all-to-all-done.13.own_back_ref), channel_id=1, source_target_pairs={{0,1},{1,0},{2,3},{3,2},{4,5},{5,4},{6,7},{7,6},{8,9},{9,8},{10,11... | collective-permute-start | bytes 3145736 | tf_op jit(solution)/shard_map/ppermute | solution.py:831
  810.5 86.0 %copy-start.48 = (bf16[128,256]{1,0:T(8,128)(2,1)}, bf16[128,256]{1,0:T(8,128)(2,1)S(1)}, u32[]{:S(2)}) copy-start(bf16[128,256]{1,0:T(8,128)(2,1)S(1)} %reduce_sum.178) | copy-start | bytes 196612
  886.5 129.7 %all-to-all-start.11 = ((bf16[8,128,256]{1,2,0:T(8,128)(2,1)}), bf16[8,128,256]{1,2,0:T(8,128)(2,1)}, u32[]{:S(2)}, u32[]{:S(2)}) async-start(bf16[8,128,256]{1,2,0:T(8,128)(2,1)} %bitcast.335), calls=%async_computation.12 | async-start | bytes 1048576 | tf_op jit(solution)/shard_map/all_to_all | solution.py:822
  899.9 137.8 %collective-permute-start.7 = (bf16[2,8,48,1024]{3,2,1,0:T(8,128)(2,1)}, bf16[2,8,48,1024]{3,2,1,0:T(8,128)(2,1)}, u32[]{:S(2)}, u32[]{:S(2)}) collective-permute-start(bf16[2,8,48,1024]{3,2,1,0:T(8,128)(2,1)} %dynamic-slice_bitcast_fusion.2), channel_id=1, source_target_pairs={{0,1},{1,0},{2,3},{3,2},{4,5},{5,4},{6,7},{7,6},{8,9},{9,8},{10,11... | collective-permute-start | bytes 4718600 | tf_op jit(solution)/shard_map/ppermute | solution.py:787
  900.0 117.4 %copy-start.15 = (f32[256,1024]{1,0:T(8,128)S(1)}, f32[256,1024]{1,0:T(8,128)}, u32[]{:S(2)}) copy-start(f32[256,1024]{1,0:T(8,128)} %param.29) | copy-start | bytes 3145732
  1015.6 34.2 %collective-permute-start.10 = (bf16[8,192,1024]{2,1,0:T(8,128)(2,1)}, bf16[8,192,1024]{2,1,0:T(8,128)(2,1)}, u32[]{:S(2)}, u32[]{:S(2)}) collective-permute-start(bf16[8,192,1024]{2,1,0:T(8,128)(2,1)} %get-tuple-element.96), channel_id=1, source_target_pairs={{0,1},{1,0},{2,3},{3,2},{4,5},{5,4},{6,7},{7,6},{8,9},{9,8},{10,11... | collective-permute-start | bytes 9437192 | tf_op jit(solution)/shard_map/ppermute | solution.py:844
  1018.3 25.4 %all-to-all-start.12 = ((bf16[4,128,256]{2,1,0:T(8,128)(2,1)}), bf16[4,128,256]{2,1,0:T(8,128)(2,1)S(1)}, u32[]{:S(2)}, u32[]{:S(2)}) async-start(bf16[4,128,256]{2,1,0:T(8,128)(2,1)} %bitcast.380), calls=%async_computation.13 | async-start | bytes 524288 | tf_op jit(solution)/shard_map/all_to_all | solution.py:827
  1043.7 12.3 copy-start.37
  1043.7 39.6 %all-to-all-start.7 = ((bf16[16,48,1024]{2,1,0:T(8,128)(2,1)}), bf16[16,48,1024]{2,1,0:T(8,128)(2,1)}, u32[]{:S(2)}, u32[]{:S(2)}) async-start(bf16[16,48,1024]{2,1,0:T(8,128)(2,1)} %bitcast.358), calls=%async_computation.7 | async-start | bytes 3145728 | tf_op jit(solution)/shard_map/all_to_all | solution.py:789
  1083.3 77.2 %all-to-all-start.14 = ((bf16[8,192,1024]{2,1,0:T(8,128)(2,1)}), bf16[8,192,1024]{2,1,0:T(8,128)(2,1)}, u32[]{:S(2)}, u32[]{:S(2)}) async-start(bf16[8,192,1024]{2,1,0:T(8,128)(2,1)} %add_convert_fusion), calls=%async_computation.15 | async-start | bytes 6291456 | tf_op jit(solution)/shard_map/all_to_all | solution.py:845
  1160.5 13.5 %all-to-all-start.8 = ((bf16[8,144,128]{2,1,0:T(8,128)(2,1)}), bf16[8,144,128]{2,1,0:T(8,128)(2,1)}, u32[]{:S(2)}, u32[]{:S(2)}) async-start(bf16[8,144,128]{2,1,0:T(8,128)(2,1)} %bitcast_bitcast_fusion.1), calls=%async_computation.8 | async-start | bytes 589824 | tf_op jit(solution)/shard_map/all_to_all | solution.py:712
  1164.6 14.2 %copy-start.28 = (f32[128,768]{1,0:T(8,128)S(1)}, f32[128,768]{1,0:T(8,128)}, u32[]{:S(2)}) copy-start(f32[128,768]{1,0:T(8,128)} %param.23) | copy-start | bytes 1179652
  1174.0 42.9 %all-to-all-start.9 = ((bf16[8,816,128]{2,1,0:T(8,128)(2,1)}), bf16[8,816,128]{2,1,0:T(8,128)(2,1)}, u32[]{:S(2)}, u32[]{:S(2)}) async-start(bf16[8,816,128]{2,1,0:T(8,128)(2,1)} %bitcast.67), calls=%async_computation.10 | async-start | bytes 3342336 | tf_op jit(solution)/shard_map/all_to_all | solution.py:712
  1223.2 30.2 %collective-permute-start.11 = (bf16[2,8,48,1024]{3,2,1,0:T(8,128)(2,1)S(1)}, bf16[2,8,48,1024]{3,2,1,0:T(8,128)(2,1)S(1)}, u32[]{:S(2)}, u32[]{:S(2)}) collective-permute-start(bf16[2,8,48,1024]{3,2,1,0:T(8,128)(2,1)S(1)} %dynamic-slice_bitcast_fusion.1), channel_id=1, source_target_pairs={{0,1},{1,0},{2,3},{3,2},{4,5},{5,4},{6,7},{7,6},{8,9},{9,8},{10,11... | collective-permute-start | bytes 4718600 | tf_op jit(solution)/shard_map/ppermute | solution.py:787
  1239.4 12.0 copy-start.32
  1239.4 12.0 copy-start.34
  1239.5 12.9 copy-start.23
  1240.1 30.5 %collective-permute-start.12 = (f32[2,1024]{1,0:T(2,128)}, f32[2,1024]{1,0:T(2,128)S(1)}, u32[]{:S(2)}, u32[]{:S(2)}) collective-permute-start(f32[2,1024]{1,0:T(2,128)} %pad_maximum_fusion.4), channel_id=1, source_target_pairs={{0,1},{1,0},{2,3},{3,2},{4,5},{5,4},{6,7},{7,6},{8,9},{9,8},{10,11... | collective-permute-start | bytes 24584 | tf_op jit(solution)/shard_map/ppermute | solution.py:899
  1255.5 9.1 copy-start.57
  1255.5 9.1 copy-start.66
  1255.5 67.7 %all-to-all-start.15 = ((bf16[16,48,1024]{2,1,0:T(8,128)(2,1)}), bf16[16,48,1024]{2,1,0:T(8,128)(2,1)}, u32[]{:S(2)}, u32[]{:S(2)}) async-start(bf16[16,48,1024]{2,1,0:T(8,128)(2,1)} %bitcast.357), calls=%async_computation.16 | async-start | bytes 3145728 | tf_op jit(solution)/shard_map/all_to_all | solution.py:789
  1264.6 55.0 %copy-start.49 = (f32[128,256]{0,1:T(8,128)S(1)}, f32[128,256]{0,1:T(8,128)}, u32[]{:S(2)}) copy-start(f32[128,256]{0,1:T(8,128)} %copy.158) | copy-start | bytes 393220
  1270.2 54.8 %copy-start.4 = (bf16[1,8,4,32,1024]{4,3,0,2,1:T(8,128)(2,1)S(1)}, bf16[1,8,4,32,1024]{4,3,0,2,1:T(8,128)(2,1)}, u32[]{:S(2)}) copy-start(bf16[1,8,4,32,1024]{4,3,0,2,1:T(8,128)(2,1)} %get-tuple-element.205) | copy-start | bytes 6291460
  1270.5 55.0 %copy-start.41 = (f32[48,1024]{1,0:T(8,128)S(1)}, f32[48,1024]{1,0:T(8,128)}, u32[]{:S(2)}) copy-start(f32[48,1024]{1,0:T(8,128)} %get-tuple-element.101) | copy-start | bytes 589828
  1270.5 55.0 %copy-start.42 = (f32[48,1024]{1,0:T(8,128)S(1)}, f32[48,1024]{1,0:T(8,128)}, u32[]{:S(2)}) copy-start(f32[48,1024]{1,0:T(8,128)} %get-tuple-element.100) | copy-start | bytes 589828
  1270.6 48.9 %collective-permute-start.13 = (f32[2,1024]{1,0:T(2,128)S(1)}, f32[2,1024]{1,0:T(2,128)S(1)}, u32[]{:S(2)}, u32[]{:S(2)}) collective-permute-start(f32[2,1024]{1,0:T(2,128)S(1)} %fusion.113), channel_id=1, source_target_pairs={{0,2},{2,0},{1,3},{3,1},{4,6},{6,4},{5,7},{7,5},{8,10},{10,8},{9,1... | collective-permute-start | bytes 24584 | tf_op jit(solution)/shard_map/ppermute | solution.py:899
  1319.5 3.7 collective-permute-start.14
  1323.2 8.5 collective-permute-start.15
  1325.0 10.4 copy-start.46
  1325.5 14.3 %copy-start.53 = (bf16[8,48,128]{2,1,0:T(8,128)(2,1)S(1)}, bf16[8,48,128]{2,1,0:T(8,128)(2,1)}, u32[]{:S(2)}) copy-start(bf16[8,48,128]{2,1,0:T(8,128)(2,1)} %get-tuple-element.104) | copy-start | bytes 294916
  1326.3 13.7 %copy-start.30 = (f32[128,768]{0,1:T(8,128)S(1)}, f32[128,768]{0,1:T(8,128)}, u32[]{:S(2)}) copy-start(f32[128,768]{0,1:T(8,128)} %copy.157) | copy-start | bytes 1179652
  1327.1 12.8 all-to-all-start.16
  1330.9 10.9 copy-start.52
  1332.5 6.0 collective-permute-start.16
  (48 other events, 206.5 us)
Sparse Core Ops, SparseCore 0:
  11.5 73.2 all-gather.6
  176.8 192.6 all-gather.8
  419.3 84.8 all-gather.10
  618.0 213.9 reduce-scatter.1
